TPU v7x, 256 devices: a whole 4x4x8 slice. The times are simulated.
256 devices in a mesh: row: 32 (over z_lo, y, core), aisle: 8 (over z_hi, x).
Axes of the slice: x: 4, y: 4, z: 8 (z_hi: 2, z_lo: 4; z = z_hi * 4 + z_lo), core: 2. Of those that a mesh axis runs over, the one named last changes fastest.
Arguments:
- tokens: bfloat16 [96, 128, 4, 512], P('row', 'aisle'), may hold values from -8 to 8
- ln_gain: float32 [512], replicated, may hold values from 0.1 to 1.9
- w_qkv: bfloat16 [512, 1536], replicated, may hold values from -2 to 2
- w_out: bfloat16 [512, 512], replicated, may hold values from -0.75 to 0.75
- w_rec: bfloat16 [512, 6912], replicated, may hold values from -0.25 to 0.25
- solid_top: int32 [768, 1024], P('row', 'aisle'), may hold values from -32 to 32
Outputs:
- flow_field: bfloat16 [4, 32, 768, 1024], P(None, None, 'row', 'aisle')
All inputs are finite; a program needn't handle non-finite values.
Results may differ from a plain program's by a relative error of at most 0.0075.
Values may be sent and summed in bfloat16 or wider, within the bound.
A program may use at most 128 MiB of HBM per device.

v0:
```python
import math

import jax
import jax.numpy as jnp
from jax import lax
from jax.sharding import PartitionSpec as P

HEADS = 8


EPSILON = 1e-05


def from_behind(value, axis, steps):
    count = lax.axis_size(axis)
    initial, last = (max(0, -steps), min(count, count - steps))
    return lax.ppermute(value, axis, [(source, source + steps) for source in range(initial, last)])


def layer_norm(values, scaling):
    widened = values.astype(jnp.float32)
    center = widened - jnp.mean(widened, axis=-1, keepdims=True)
    spread = jnp.mean(center * center, axis=-1, keepdims=True)
    return (center * lax.rsqrt(spread + EPSILON) * scaling).astype(jnp.bfloat16)


def attend(block):
    rows_here, lines_here, triple = block.shape
    model_width = triple // 3
    head_dim = model_width // HEADS
    query_part = block[:, :, :model_width].reshape(rows_here, lines_here, HEADS, head_dim)
    key_part = block[:, :, model_width : 2 * model_width].reshape(
        rows_here, lines_here, HEADS, head_dim
    )
    value_part = block[:, :, 2 * model_width :].reshape(rows_here, lines_here, HEADS, head_dim)
    scores = jnp.einsum(
        "rnhd,snhd->nhrs", query_part, key_part, preferred_element_type=jnp.float32
    ) / math.sqrt(head_dim)
    weights = jax.nn.softmax(scores, axis=-1).astype(jnp.bfloat16)
    blended = jnp.einsum("nhrs,snhd->rnhd", weights, value_part, preferred_element_type=jnp.float32)
    return blended.astype(jnp.bfloat16).reshape(rows_here, lines_here, model_width)


def attend_items(block):
    return attend(block[:, 0])[:, None]


def placement(count):
    flat = lax.broadcasted_iota(jnp.int32, (count * 12, 8 * count + 4), 0)
    target = lax.broadcasted_iota(jnp.int32, (count * 12, 8 * count + 4), 1)
    return jnp.where(target == 8 * (flat // 12) + flat % 12, 1.0, 0.0).astype(jnp.float32)


def fold_pair(stacked, token_axis, offset_axis):
    lower = lax.slice_in_dim(stacked, 0, 8, axis=offset_axis)
    upper = lax.slice_in_dim(stacked, 8, 12, axis=offset_axis)
    pad_lower = [(0, 0)] * stacked.ndim
    pad_lower[token_axis] = (0, 1)
    pad_upper = [(0, 0)] * stacked.ndim
    pad_upper[token_axis] = (1, 0)
    pad_upper[offset_axis] = (0, 4)
    return jnp.pad(lower, pad_lower) + jnp.pad(upper, pad_upper)


def recover(tile, w_rec):
    rows_here, cols_here, levels_here, model_width = tile.shape
    fields = w_rec.shape[1] // 1728
    inner = fields * 144
    reordered = (
        w_rec.reshape(model_width, inner, 12).swapaxes(1, 2).reshape(model_width, 12 * inner)
    )
    ordered_tokens = tile.transpose(0, 2, 1, 3).reshape(-1, model_width)
    patches = jnp.dot(ordered_tokens, reordered, preferred_element_type=jnp.float32)
    patches = patches.reshape(rows_here * levels_here, cols_here * 12, inner)
    across = placement(cols_here)
    spread_y = lax.dot_general(
        patches, across, (((1,), (0,)), ((), ())), precision=lax.Precision.HIGHEST
    )
    width_y = 8 * cols_here + 4
    spread_y = spread_y.reshape(rows_here, levels_here, fields, 12, 12, width_y)
    folded_x = fold_pair(spread_y, 0, 4)
    folded_z = fold_pair(folded_x, 1, 3)
    arranged = folded_z.transpose(2, 1, 3, 0, 4, 5)
    arranged = arranged.reshape(fields, 8 * levels_here + 8, 8 * rows_here + 8, width_y)
    return arranged[:, 2 : 2 + 8 * levels_here, : 8 * rows_here + 4]


def body(tokens, ln_gain, w_qkv, w_out, w_rec, solid_top):
    row_tokens, aisle_tokens, height_tokens, model_width = tokens.shape
    groups = lax.axis_size("row")
    per_group = aisle_tokens * height_tokens // groups
    normed = layer_norm(tokens, ln_gain)
    projected_all = jnp.dot(
        normed.reshape(-1, model_width), w_qkv, preferred_element_type=jnp.float32
    ).astype(jnp.bfloat16)
    projected_all = projected_all.reshape(row_tokens, groups, per_group, 3 * model_width)
    attended = attend_items(
        lax.all_to_all(projected_all, "row", split_axis=1, concat_axis=0, tiled=True)
    )
    attended = lax.all_to_all(attended, "row", split_axis=0, concat_axis=1, tiled=True)
    branch = jnp.dot(attended.reshape(-1, model_width), w_out, preferred_element_type=jnp.float32)
    block_out = (tokens.reshape(-1, model_width).astype(jnp.float32) + branch).astype(jnp.bfloat16)
    block_out = block_out.reshape(row_tokens, aisle_tokens, height_tokens, model_width)
    canvas = recover(block_out, w_rec)
    from_lower = from_behind(canvas[:, :, -2:, :].astype(jnp.bfloat16), "row", 1).astype(
        jnp.float32
    )
    from_upper = from_behind(canvas[:, :, :2, :].astype(jnp.bfloat16), "row", -1).astype(
        jnp.float32
    )
    middle = canvas[:, :, 2:-2, :]
    middle = middle.at[:, :, :2, :].add(from_lower).at[:, :, -2:, :].add(from_upper)
    from_left = from_behind(middle[..., -2:], "aisle", 1)
    from_right = from_behind(middle[..., :2], "aisle", -1)
    cells = middle[..., 2:-2].at[..., :2].add(from_left).at[..., -2:].add(from_right)
    levels = lax.broadcasted_iota(jnp.int32, (8 * height_tokens, 1, 1), 0)
    inside_rack = levels < solid_top[None, :, :]
    return jnp.where(inside_rack[None], 0.0, cells).astype(jnp.bfloat16)


def solution(mesh):
    in_specs = (P("row", "aisle", None, None), P(), P(), P(), P(), P("row", "aisle"))
    out_specs = P(None, None, "row", "aisle")
    return jax.shard_map(body, mesh=mesh, in_specs=in_specs, out_specs=out_specs, check_vma=False)
```

profile of v0, /device:TPU:217, one launch (start us, length us, event | category | flops | bytes accessed | tf_op | source)
XLA Modules:
  0.0 204.4 jit_solution(11109478334483197029)
XLA Ops:
  0.0 1.2 convert_reduce_fusion
  1.2 1.2 multiply_reduce_fusion
  2.4 1.1 multiply_convert_fusion
  4.8 21.2 %all_to_all.30 = bf16[3,32,2,1536]{3,2,0,1:T(2,128)(2,1)S(1)} all-to-all(bf16[3,32,2,1536]{3,2,0,1:T(2,128)(2,1)S(1)} %copy.21), channel_id=1, replica_groups=mesh['row'=32,'aisle'=8] {'row'}, dimensions={1} | all-to-all | bytes 1179648 | tf_op jit(solution)/shard_map/all_to_all | solution.py:98
  28.2 0.8 copy.26
  29.0 8.0 %all-to-all-start.1 = ((bf16[96,1,2,512]{3,2,1,0:T(2,128)(2,1)}), bf16[96,1,2,512]{3,2,1,0:T(2,128)(2,1)S(1)}, u32[]{:S(2)}, u32[]{:S(2)}) async-start(bf16[96,1,2,512]{3,2,1,0:T(2,128)(2,1)} %copy.26), calls=%async_computation.1 | async-start | bytes 393216 | tf_op jit(solution)/shard_map/all_to_all | solution.py:100
  37.0 10.3 %copy.29 = bf16[512,6912]{0,1:T(8,128)(2,1)} copy(bf16[512,6912]{1,0:T(8,128)(2,1)} %param.18) | data formatting | bytes 14155776 | tf_op args[4]
  47.4 12.1 %reshape.207 = bf16[512,576,12]{0,2,1:T(8,128)(2,1)} reshape(bf16[512,6912]{0,1:T(8,128)(2,1)} %copy.29) | data formatting | bytes 14155776 | tf_op jit(solution)/shard_map/reshape | solution.py:70
  59.4 10.6 %copy.30 = bf16[512,12,576]{0,2,1:T(8,128)(2,1)} copy(bf16[512,12,576]{0,1,2:T(8,128)(2,1)} %bitcast.45) | data formatting | bytes 14155776 | tf_op jit(solution)/shard_map/transpose | solution.py:70
  70.6 7.8 %fusion.30 = f32[192,6912]{1,0:T(8,128)} fusion(bf16[192,512]{1,0:T(8,128)(2,1)S(1)} %bitcast.57, bf16[512,6912]{0,1:T(8,128)(2,1)} %bitcast.49), kind=kOutput, calls=%fused_computation.55 | convolution fusion | flops 1358954496 | bytes 12582912 | tf_op jit(solution)/shard_map/dot_general | solution.py:73
  78.4 7.7 %reshape.209 = f32[12,192,576]{2,1,0:T(8,128)} reshape(f32[192,6912]{1,0:T(8,128)} %fusion.30) | data formatting | bytes 10616832 | tf_op jit(solution)/shard_map/reshape | solution.py:74
  86.1 8.0 %copy.31 = f32[12,192,576]{1,2,0:T(8,128)} copy(f32[12,192,576]{2,1,0:T(8,128)} %reshape.209) | data formatting | bytes 10616832 | tf_op jit(solution)/shard_map/reshape | solution.py:74
  94.0 8.7 %dot_general.28 = f32[3,4,4,12,12,192]{5,4,3,2,1,0:T(8,128)} reshape(f32[12,576,192]{2,1,0:T(8,128)} %bitcast.50) | data formatting | bytes 10616832 | tf_op jit(solution)/shard_map/dot_general | solution.py:76
  102.8 10.3 %fusion.7 = f32[3,4,4,12,12,132]{5,4,3,2,1,0:T(8,128)S(1)} fusion(f32[3,4,4,12,12,192]{5,4,3,2,1,0:T(8,128)} %dot_general.28, s32[192]{0:T(256)S(1)} %get-tuple-element.62, s32[192]{0:T(256)S(1)} %get-tuple-element.65, s32[192]{0:T(256)S(1)} %get-tuple-element.61, s32[192]{0:T(256)S(1)} %get-tuple-element.66, pred[192]{0:T(512)(128)(4,1)S(1)} %get-tuple-element.63, ...), kind=kOutput, calls=%fused_computation.23 | convolution fusion | flops 2102284800 | bytes 8961408 | tf_op jit(solution)/shard_map/dot_general | solution.py:76
  113.0 0.7 slice.183
  114.4 0.7 fusion.1
  116.0 0.8 copy.32
  117.5 3.4 %collective-permute-start = (bf16[4,32,2,132]{3,2,1,0:T(2,128)(2,1)S(1)}, bf16[4,32,2,132]{3,2,1,0:T(2,128)(2,1)S(1)}, u32[]{:S(2)}, u32[]{:S(2)}) collective-permute-start(bf16[4,32,2,132]{3,2,1,0:T(2,128)(2,1)S(1)} %get-tuple-element.57), channel_id=1, source_target_pairs={{0,8},{8,16},{16,24},{24,32},{32,40},{40,48},{48,56},{56,64},{64,7... | collective-permute-start | bytes 202760 | tf_op jit(solution)/shard_map/ppermute | solution.py:17
  121.2 1.9 collective-permute-start.1
  123.5 6.2 %collective-permute-done.1 = bf16[4,32,2,132]{3,2,1,0:T(2,128)(2,1)S(1)} collective-permute-done((bf16[4,32,2,132]{3,2,1,0:T(2,128)(2,1)S(1)}, bf16[4,32,2,132]{3,2,1,0:T(2,128)(2,1)S(1)}, u32[]{:S(2)}, u32[]{:S(2)}) %collective-permute-start.1) | collective-permute-done | bytes 67616 | tf_op jit(solution)/shard_map/ppermute | solution.py:17
  130.0 2.1 %fusion.26 = (f32[4,32,24,2]{3,2,1,0:T(8,128)S(1)}, f32[4,32,24,2]{3,2,1,0:T(8,128)}, f32[4,32,24,2]{3,2,1,0:T(8,128)S(1)}) fusion(f32[4,32,24,132]{3,2,1,0:T(8,128)S(1)} %fusion.5), kind=kLoop, calls=%fused_computation.51 | loop fusion | bytes 147456 | tf_op jit(solution)/shard_map/slice | solution.py:114
  132.2 2.1 %copy.33 = f32[4,32,24,2]{1,2,3,0:T(8,128)S(1)} copy(f32[4,32,24,2]{3,2,1,0:T(8,128)} %get-tuple-element.54) | data formatting | bytes 49152 | tf_op jit(solution)/shard_map/slice | solution.py:113
  134.2 3.1 %collective-permute-start.2 = (f32[4,32,24,2]{1,2,3,0:T(8,128)S(1)}, f32[4,32,24,2]{1,2,3,0:T(8,128)}, u32[]{:S(2)}, u32[]{:S(2)}) collective-permute-start(f32[4,32,24,2]{1,2,3,0:T(8,128)S(1)} %copy.33), channel_id=1, source_target_pairs={{0,1},{1,2},{2,3},{3,4},{4,5},{5,6},{6,7},{8,9},{9,10},{10,11},{11... | collective-permute-start | bytes 73736 | tf_op jit(solution)/shard_map/ppermute | solution.py:17
  138.0 8.4 %collective-permute-start.3 = (f32[4,32,24,2]{1,2,3,0:T(8,128)S(1)}, f32[4,32,24,2]{1,2,3,0:T(8,128)}, u32[]{:S(2)}, u32[]{:S(2)}) collective-permute-start(f32[4,32,24,2]{1,2,3,0:T(8,128)S(1)} %copy.36), channel_id=1, source_target_pairs={{1,0},{2,1},{3,2},{4,3},{5,4},{6,5},{7,6},{9,8},{10,9},{11,10},{12... | collective-permute-start | bytes 73736 | tf_op jit(solution)/shard_map/ppermute | solution.py:17
  146.5 2.4 %slice.192 = f32[4,32,24,128]{3,2,1,0:T(8,128)S(1)} slice(f32[4,32,24,132]{3,2,1,0:T(8,128)} %copy-done.2), slice={[0:4], [0:32], [0:24], [2:130]} | slice | bytes 3145728 | tf_op jit(solution)/shard_map/slice | solution.py:115
  149.5 0.9 add.77
  150.4 0.7 copy.35
  151.1 18.0 %scatter-add.16 = f32[4,32,24,128]{3,2,1,0:T(8,128)S(1)} dynamic-update-slice(f32[4,32,24,128]{3,2,1,0:T(8,128)S(1)} %slice.192, f32[4,32,24,2]{3,2,1,0:T(8,128)S(1)} %copy.35, s32[]{:T(128)} %constant.141.clone.1, s32[]{:T(128)} %constant.141.clone.1, s32[]{:T(128)} %constant.141.clone.1, s32[]{:T(128)} %constant.141.clone.1) | dynamic-update-slice | bytes 49156 | tf_op jit(solution)/shard_map/scatter-add | solution.py:115
  170.2 0.9 add.78
  171.1 1.8 copy.38
  172.9 30.4 %scatter-add.19 = f32[4,32,24,128]{3,2,1,0:T(8,128)S(1)} dynamic-update-slice(f32[4,32,24,128]{3,2,1,0:T(8,128)S(1)} %scatter-add.16, f32[4,32,24,2]{3,2,1,0:T(8,128)} %copy.38, s32[]{:T(128)} %constant.141.clone.1, s32[]{:T(128)} %constant.141.clone.1, s32[]{:T(128)} %constant.141.clone.1, s32[]{:T(128)} %constant.146.clone.1) | dynamic-update-slice | bytes 49156 | tf_op jit(solution)/shard_map/scatter-add | solution.py:115
  203.3 1.0 select_convert_fusion
  (51 shorter events, 9.7 us)
Async XLA Ops:
  0.0 3.6 %copy-start = (bf16[512,1536]{1,0:T(8,128)(2,1)S(1)}, bf16[512,1536]{1,0:T(8,128)(2,1)}, u32[]{:S(2)}) copy-start(bf16[512,1536]{1,0:T(8,128)(2,1)} %param.16) | copy-start | bytes 4718596
  27.2 9.8 %copy-start.3 = (bf16[3,16,4,512]{3,2,1,0:T(4,128)(2,1)S(1)}, bf16[3,16,4,512]{3,2,1,0:T(4,128)(2,1)}, u32[]{:S(2)}) copy-start(bf16[3,16,4,512]{3,2,1,0:T(4,128)(2,1)} %param.14) | copy-start | bytes 589828
  29.0 41.0 %all-to-all-start.1 = ((bf16[96,1,2,512]{3,2,1,0:T(2,128)(2,1)}), bf16[96,1,2,512]{3,2,1,0:T(2,128)(2,1)S(1)}, u32[]{:S(2)}, u32[]{:S(2)}) async-start(bf16[96,1,2,512]{3,2,1,0:T(2,128)(2,1)} %copy.26), calls=%async_computation.1 | async-start | bytes 393216 | tf_op jit(solution)/shard_map/all_to_all | solution.py:100
  59.4 10.8 %copy-start.4 = (bf16[512,512]{1,0:T(8,128)(2,1)S(1)}, bf16[512,512]{1,0:T(8,128)(2,1)}, u32[]{:S(2)}) copy-start(bf16[512,512]{1,0:T(8,128)(2,1)} %param.17) | copy-start | bytes 1572868
  117.5 5.7 %collective-permute-start = (bf16[4,32,2,132]{3,2,1,0:T(2,128)(2,1)S(1)}, bf16[4,32,2,132]{3,2,1,0:T(2,128)(2,1)S(1)}, u32[]{:S(2)}, u32[]{:S(2)}) collective-permute-start(bf16[4,32,2,132]{3,2,1,0:T(2,128)(2,1)S(1)} %get-tuple-element.57), channel_id=1, source_target_pairs={{0,8},{8,16},{16,24},{24,32},{32,40},{40,48},{48,56},{56,64},{64,7... | collective-permute-start | bytes 202760 | tf_op jit(solution)/shard_map/ppermute | solution.py:17
  121.2 8.4 %collective-permute-start.1 = (bf16[4,32,2,132]{3,2,1,0:T(2,128)(2,1)S(1)}, bf16[4,32,2,132]{3,2,1,0:T(2,128)(2,1)S(1)}, u32[]{:S(2)}, u32[]{:S(2)}) collective-permute-start(bf16[4,32,2,132]{3,2,1,0:T(2,128)(2,1)S(1)} %get-tuple-element.56), channel_id=1, source_target_pairs={{8,0},{16,8},{24,16},{32,24},{40,32},{48,40},{56,48},{64,56},{72,6... | collective-permute-start | bytes 202760 | tf_op jit(solution)/shard_map/ppermute | solution.py:17
  130.0 2.1 %copy-start.2 = (f32[4,32,24,132]{3,2,1,0:T(8,128)}, f32[4,32,24,132]{3,2,1,0:T(8,128)S(1)}, u32[]{:S(2)}) copy-start(f32[4,32,24,132]{3,2,1,0:T(8,128)S(1)} %fusion.5) | copy-start | bytes 4866052
  132.1 14.3 %copy-start.5 = (s32[24,128]{1,0:T(8,128)S(1)}, s32[24,128]{1,0:T(8,128)}, u32[]{:S(2)}) copy-start(s32[24,128]{1,0:T(8,128)} %param.19) | copy-start | bytes 36868
  134.2 15.3 %collective-permute-start.2 = (f32[4,32,24,2]{1,2,3,0:T(8,128)S(1)}, f32[4,32,24,2]{1,2,3,0:T(8,128)}, u32[]{:S(2)}, u32[]{:S(2)}) collective-permute-start(f32[4,32,24,2]{1,2,3,0:T(8,128)S(1)} %copy.33), channel_id=1, source_target_pairs={{0,1},{1,2},{2,3},{3,4},{4,5},{5,6},{6,7},{8,9},{9,10},{10,11},{11... | collective-permute-start | bytes 73736 | tf_op jit(solution)/shard_map/ppermute | solution.py:17
  138.0 32.2 %collective-permute-start.3 = (f32[4,32,24,2]{1,2,3,0:T(8,128)S(1)}, f32[4,32,24,2]{1,2,3,0:T(8,128)}, u32[]{:S(2)}, u32[]{:S(2)}) collective-permute-start(f32[4,32,24,2]{1,2,3,0:T(8,128)S(1)} %copy.36), channel_id=1, source_target_pairs={{1,0},{2,1},{3,2},{4,3},{5,4},{6,5},{7,6},{9,8},{10,9},{11,10},{12... | collective-permute-start | bytes 73736 | tf_op jit(solution)/shard_map/ppermute | solution.py:17
  171.1 33.2 %copy-start.1 = (bf16[512,1536]{1,0:T(8,128)(2,1)S(1)}, bf16[512,1536]{1,0:T(8,128)(2,1)}, u32[]{:S(2)}) copy-start(bf16[512,1536]{1,0:T(8,128)(2,1)} %param.16) | copy-start | bytes 4718596
where the time goes:
time: 206 us; the launch traced here: 204 us
  local copies, waits for them, and re-layouts  123 us (60%)
  starting transfers between devices  24.8 us (12%)
  blocking collectives  21.2 us (10%)
  matrix products  19.8 us (10%)
  other arithmetic  9.2 us (4%)
  waiting for transfers between devices  6.17 us (3%)
    scatter-add x2, local copies, waits for them, and re-layouts, body(): middle[..., 2:-2].at[..., :2].add(from_left).at[..., -2:].add(from_right)  48.3 us
    all_to_all x1, blocking collectives, body(): lax.all_to_all(projected_all, 'row', split_axis=1, concat_axis=0, tiled=T...  21.2 us
    ppermute x4, starting transfers between devices, from_behind(): lax.ppermute(value, axis, [(source, source + steps) for source in range(i...  16.8 us
    reshape x2, local copies, waits for them, and re-layouts, recover(): patches = patches.reshape(rows_here * levels_here, cols_here * 12, inner)  15.6 us
    reshape x1, local copies, waits for them, and re-layouts, recover(): w_rec.reshape(model_width, inner, 12).swapaxes(1, 2)  12.1 us
    transpose x1, local copies, waits for them, and re-layouts, recover(): w_rec.reshape(model_width, inner, 12).swapaxes(1, 2)  10.6 us
    unnamed x13, local copies, waits for them, and re-layouts  10.3 us
    dot_general x1, matrix products, recover(): lax.dot_general(patches, across, (((1,), (0,)), ((), ())), precision=lax....  10.3 us
  transfers between devices with their start and end apart: 5, of which 1 were waited for; matrix products, arithmetic and copies ran while one was open for 28% of the time, Pallas kernels for 0%

commit v1 on v0

v1 whole, which is shorter than its diff:
```python
import jax
import jax.numpy as jnp
from jax import lax
from jax.experimental import pallas as pl
from jax.experimental.pallas import tpu as pltpu
from jax.sharding import PartitionSpec as P

EPSILON = 1e-05
N_ROW, N_AISLE = 32, 8
D, HEADS, DH = 512, 8, 64
MESH = pl.DeviceIdType.MESH
F32, BF16, I32 = jnp.float32, jnp.bfloat16, jnp.int32


def iota(shape, dim):
    return lax.broadcasted_iota(I32, shape, dim)


def one_hot(hit):
    return jnp.where(hit, 1.0, 0.0).astype(BF16)


def dot(a, b):
    return lax.dot_general(a, b, (((1,), (0,)), ((), ())), preferred_element_type=F32)


def dot_nt(a, b):
    return lax.dot_general(a, b, (((1,), (1,)), ((), ())), preferred_element_type=F32)


def send_selector():
    row = iota((256, 1), 0)
    source = (row & 3) * 64 + (row >> 3) * 2 + ((row >> 2) & 1)
    source = jnp.where((row & 3) < 3, source, -1)
    return one_hot(iota((256, 192), 1) == source)


def weight_selector(step):
    row = iota((192, 1), 0)
    main = ((row & 7) + 2) * 12 + (row >> 3) + 2
    below = ((row & 7) + 2) * 12 + ((row >> 3) & 1) + 10
    above = ((row & 7) + 2) * 12 + ((row >> 3) & 1)
    edge = row - 96
    side = jnp.where(edge >= 48, 1, 0)
    edge = edge - 48 * side
    part = edge >> 4
    y = (edge >> 1) & 7
    x = edge & 1
    kx = jnp.where(side == 0, x + 10, x)
    ky = jnp.where(
        part == 0,
        y + 2,
        jnp.where(
            part == 1, jnp.where(y < 2, y + 10, -999), jnp.where(y >= 6, y - 6, -999)
        ),
    )
    edged = kx * 12 + ky
    column = jnp.where(row < 64, main, jnp.where(row < 80, below, jnp.where(row < 96, above, edged)))
    return one_hot(iota((192, 256), 1) - 16 * step == column)


def halo_selector(da, row_index, aisle_index):
    q = iota((384, 1), 0)
    h = jnp.where(q >= 288, 3, jnp.where(q >= 192, 2, jnp.where(q >= 96, 1, 0)))
    rest = q - 96 * h
    r = (rest >> 4) - 1
    a = (rest & 15) + da
    inside = jnp.where(
        r < 0, 256 + a * 4 + h, jnp.where(r > 2, 320 + a * 4 + h, a * 16 + h * 4 + r)
    )
    left = jnp.where(r < 0, 416 + h * 4 + 2, jnp.where(r > 2, 448 + h * 4, 384 + h * 4 + r))
    right = jnp.where(r < 0, 432 + h * 4 + 2, jnp.where(r > 2, 464 + h * 4, 400 + h * 4 + r))
    source = jnp.where(a < 0, left, jnp.where(a > 15, right, inside))
    absent = (
        (r > 3)
        | ((r < 0) & (row_index == 0))
        | ((r > 2) & (row_index == N_ROW - 1))
        | ((a < 0) & (aisle_index == 0))
        | ((a > 15) & (aisle_index == N_AISLE - 1))
    )
    source = jnp.where(absent, -1, source)
    return one_hot(iota((384, 512), 1) == source)


def lane_permutation():
    row = iota((1024, 1), 0)
    r = (row >> 4) & 3
    target = ((row >> 6) & 1) * 384 + r * 128 + (row & 15) * 8 + (row >> 7)
    target = jnp.where(r < 3, target, -1)
    return one_hot(iota((1024, 768), 1) == target)


def edge_selector():
    column = iota((1, 256), 1)
    target = (
        ((column >> 1) & 7) * 64 + (column >> 5) * 8 + ((column >> 4) & 1) * 6 + (column & 1)
    )
    return one_hot(iota((512, 256), 0) == target)


def row_halo_selector():
    row = iota((128, 1), 0)
    source = (row & 63) * 4 + jnp.where(row >= 64, 2, 0)
    return one_hot(iota((128, 256), 1) == source)


def attend_lines(x, gain, w_qkv, w_out):
    center = x - jnp.mean(x, axis=-1, keepdims=True)
    spread = jnp.mean(center * center, axis=-1, keepdims=True)
    normed = (center * lax.rsqrt(spread + EPSILON) * gain).astype(BF16)
    qkv = dot(normed, w_qkv).astype(BF16)
    rows, cols = iota((256, 256), 0), iota((256, 256), 1)
    valid = (((rows ^ cols) & 4) == 0) & ((cols & 3) < 3)
    first = iota((256, 128), 1) < DH
    mask_first = one_hot(first)
    mask_second = 1 - mask_first
    parts = []
    for pair in range(HEADS // 2):
        at = pair * 2 * DH
        query = qkv[:, at : at + 2 * DH]
        key = qkv[:, D + at : D + at + 2 * DH]
        value = qkv[:, 2 * D + at : 2 * D + at + 2 * DH]
        halves = []
        for mask in (mask_first, mask_second):
            scores = dot_nt(query * mask, key) * (1.0 / 8.0)
            scores = jnp.where(valid, scores, -jnp.inf)
            grown = jnp.exp(scores - jnp.max(scores, axis=-1, keepdims=True))
            weights = grown / jnp.sum(grown, axis=-1, keepdims=True)
            halves.append(dot(weights.astype(BF16), value))
        parts.append(jnp.where(first, halves[0], halves[1]).astype(BF16))
    attended = jnp.concatenate(parts, axis=1)
    return x + dot(attended, w_out)


def kernel(
    tokens_ref, gain_ref, w_qkv_hbm, w_out_hbm, w_rec_hbm, solid_ref,
    out_ref,
    w_qkv, w_out, w_rec, send1, recv1, send2, cat, row_halo,
    w_sel, main_w, side_w, edge_w, halo_sel, perm, edge_sel, row_sel,
    shifted, acc, edge_acc, ready,
    load_sem, send_sem, recv_sem,
):
    i, k = lax.axis_index("row"), lax.axis_index("aisle")

    loads = [pltpu.make_async_copy(w_qkv_hbm, w_qkv, load_sem.at[6]),
             pltpu.make_async_copy(w_out_hbm, w_out, load_sem.at[7])]
    for load in loads:
        load.start()

    def rec_load(q):
        columns = pl.ds(pl.multiple_of(q * 1152, 1152), 1152)
        return pltpu.make_async_copy(w_rec_hbm.at[:, columns], w_rec.at[:, columns], load_sem.at[q])

    for q in range(6):
        rec_load(q).start()

    barrier = pltpu.get_barrier_semaphore()

    @pl.loop(1, N_ROW)
    def _(step):
        pl.semaphore_signal(barrier, inc=1, device_id=(lax.rem(i + step, N_ROW), k), device_id_type=MESH)

    up, down = lax.rem(i + 1, N_ROW), lax.rem(i + N_ROW - 1, N_ROW)
    right, left = lax.rem(k + 1, N_AISLE), lax.rem(k + N_AISLE - 1, N_AISLE)
    for device in ((i, right), (i, left), (up, right), (up, left), (down, right), (down, left)):
        pl.semaphore_signal(barrier, inc=1, device_id=device, device_id_type=MESH)

    send1[...] = dot(send_selector(), tokens_ref[...]).reshape(32, 8, D).astype(BF16)
    recv1[i] = send1[i]
    pl.semaphore_wait(barrier, N_ROW - 1 + 6)

    def exchange(source, target, sem):
        @pl.loop(1, N_ROW)
        def _(step):
            j = lax.rem(i + step, N_ROW)
            pltpu.make_async_remote_copy(
                src_ref=source.at[j], dst_ref=target.at[i],
                send_sem=send_sem.at[sem], recv_sem=recv_sem.at[sem],
                device_id=(j, k), device_id_type=MESH,
            ).start()

    def drain(source, target, count, sem, start=0):
        return pltpu.make_async_remote_copy(
            src_ref=source.at[pl.ds(start, count)], dst_ref=target.at[pl.ds(start, count)],
            send_sem=send_sem.at[sem], recv_sem=recv_sem.at[sem],
            device_id=(up, k), device_id_type=MESH,
        )

    exchange(send1, recv1, 0)

    @pl.loop(0, 8)
    def _(s):
        w_sel[s] = weight_selector(s)

    def prepare(q):
        rec_load(q).wait()
        for p in range(4):
            index = q * 4 + p
            c, pair = index // 6, index % 6
            found = []
            for s in (2 * p, 2 * p + 1):
                window = w_rec[:, pl.ds(pl.multiple_of(128 * (9 * q + s), 128), 256)]
                found.append(dot_nt(w_sel[s], window))
            main = [f[:64].reshape(8, 8, D) for f in found]
            main_w[c, :, pair] = jnp.concatenate(main, axis=1).astype(BF16)
            for side in range(2):
                at = 64 + 16 * side
                halves = [f[at : at + 16].reshape(2, 8, D) for f in found]
                side_w[side, c, :, pair] = jnp.concatenate(halves, axis=1).astype(BF16)
                for n in range(2):
                    for part in range(3):
                        at = 96 + 48 * side + 16 * part
                        edge_w[side, c, 2 * pair + n, :, part * D : (part + 1) * D] = found[n][at : at + 16].astype(BF16)

    @pl.loop(0, 3)
    def _(q):
        prepare(q)

    for load in loads:
        load.wait()
    drain(send1, recv1, N_ROW - 1, 0).wait_recv()

    x = recv1[...].astype(F32).reshape(256, D)
    block_out = attend_lines(x, gain_ref[...], w_qkv[...], w_out[...])
    send2[...] = block_out.reshape(32, 8, D).astype(BF16)
    cat[i] = send2[i]
    exchange(send2, cat, 1)

    row_sel[...] = row_halo_selector()
    perm[...] = lane_permutation()
    edge_sel[...] = edge_selector()
    for n, da in enumerate((0, -1, 1)):
        halo_sel[n] = halo_selector(da, i, k)
    shifted[0] = jnp.zeros(shifted.shape[1:], BF16)
    shifted[5] = jnp.zeros(shifted.shape[1:], BF16)
    cat[60:64] = jnp.zeros((4, 8, D), BF16)

    @pl.loop(3, 6)
    def _(q):
        prepare(q)

    drain(send1, recv1, N_ROW - 1, 0).wait_send()
    drain(send2, cat, N_ROW - 1, 1).wait_recv()

    own = cat[:32].astype(F32).reshape(256, D).astype(BF16)
    row_halo[...] = dot(row_sel[...], own).reshape(16, 8, D).astype(BF16)

    def halo_copy(source, at, size, device):
        pltpu.make_async_remote_copy(
            src_ref=source, dst_ref=cat.at[pl.ds(at, size)],
            send_sem=send_sem.at[2], recv_sem=recv_sem.at[2],
            device_id=device, device_id_type=MESH,
        ).start()

    lowest, highest = cat.at[pl.ds(0, 2)], cat.at[pl.ds(30, 2)]
    halo_copy(row_halo.at[pl.ds(0, 8)], 40, 8, (down, k))
    halo_copy(row_halo.at[pl.ds(8, 8)], 32, 8, (up, k))
    halo_copy(lowest, 50, 2, (i, left))
    halo_copy(highest, 48, 2, (i, right))
    halo_copy(highest, 52, 2, (up, right))
    halo_copy(lowest, 54, 2, (up, left))
    halo_copy(highest, 56, 2, (down, right))
    halo_copy(lowest, 58, 2, (down, left))
    drain(send2, cat, N_ROW - 1, 1).wait_send()
    drain(cat, cat, 28, 2, 32).wait_recv()
    drain(cat, cat, 28, 2, 32).wait_send()

    gathered = cat[...].astype(F32).reshape(512, D).astype(BF16)
    for n in range(3):
        picked = dot(halo_sel[n], gathered).reshape(4, 6, 16, D).astype(BF16)
        shifted[1:5, :, :, n * D : (n + 1) * D] = picked

    spans = ((0, 0, 8, 2), (-1, 0, 2, 10), (1, 6, 2, 0))

    @pl.loop(0, 4)
    def _(c):
        for dz, z, n, kz in spans:
            pairs = pl.ds(kz // 2, n // 2)
            here = pl.ds(1 + dz, 4)
            level = pl.ds(z, n)
            for part in range(3):
                token_part = shifted[here, 1:5, :, part * D : (part + 1) * D].reshape(256, D)
                if part == 0:
                    rows, size, y = main_w[c, :, pairs], 8, 0
                else:
                    rows, size, y = side_w[part - 1, c, :, pairs], 2, 6 * (part - 1)
                found = dot_nt(rows.reshape(-1, D), token_part).reshape(size, n, 8, 256)
                if dz == 0 and part == 0:
                    acc[c] = found
                else:
                    acc[c, pl.ds(y, size), level] += found
            for side in range(2):
                token_part = shifted[here, pl.ds(2 * side, 4)].reshape(256, 3 * D)
                rows = edge_w[side, c, pl.ds(kz, n)].reshape(-1, 3 * D)
                found = dot_nt(rows, token_part).reshape(n, 16, 256)
                if dz == 0:
                    edge_acc[c, :, side] = found
                else:
                    edge_acc[c, level, side] += found
        edges = edge_acc[c].reshape(256, 256).astype(BF16)
        total = acc[c].reshape(512, 256) + dot(edge_sel[...], edges)
        total = total.astype(BF16)
        for y in range(8):
            for b in range(2):
                ready[b, c, :, y * 128 : (y + 1) * 128] = total[y * 64 : (y + 1) * 64, b * 128 : (b + 1) * 128]

    solid = solid_ref[...]
    for h in range(4):
        b, low = h // 2, h % 2
        cells = dot(ready[b].reshape(256, 1024), perm[:, low * 384 : (low + 1) * 384])
        cells = jnp.concatenate(
            [cells[:, r * 128 : (r + 1) * 128].reshape(4, 8, 8, 128) for r in range(3)], axis=2
        )
        level = iota((4, 8, 24, 128), 1) + 8 * h
        out_ref[:, 8 * h : 8 * h + 8] = jnp.where(level < solid[None, None], 0.0, cells).astype(BF16)


def body(tokens, ln_gain, w_qkv, w_out, w_rec, solid_top):
    vmem = pl.BlockSpec(memory_space=pltpu.VMEM)
    hbm = pl.BlockSpec(memory_space=pl.ANY)
    return pl.pallas_call(
        kernel,
        out_shape=jax.ShapeDtypeStruct((4, 32, 24, 128), BF16),
        in_specs=[vmem, vmem, hbm, hbm, hbm, vmem],
        out_specs=vmem,
        scratch_shapes=[
            pltpu.VMEM((D, 3 * D), BF16),
            pltpu.VMEM((D, D), BF16),
            pltpu.VMEM((D, 6912), BF16),
            pltpu.VMEM((32, 8, D), BF16),
            pltpu.VMEM((32, 8, D), BF16),
            pltpu.VMEM((32, 8, D), BF16),
            pltpu.VMEM((64, 8, D), BF16),
            pltpu.VMEM((16, 8, D), BF16),
            pltpu.VMEM((8, 192, 256), BF16),
            pltpu.VMEM((4, 8, 6, 16, D), BF16),
            pltpu.VMEM((2, 4, 2, 6, 16, D), BF16),
            pltpu.VMEM((2, 4, 12, 16, 3 * D), BF16),
            pltpu.VMEM((3, 384, 512), BF16),
            pltpu.VMEM((1024, 768), BF16),
            pltpu.VMEM((512, 256), BF16),
            pltpu.VMEM((128, 256), BF16),
            pltpu.VMEM((6, 6, 16, 3 * D), BF16),
            pltpu.VMEM((4, 8, 8, 8, 256), F32),
            pltpu.VMEM((4, 8, 2, 16, 256), F32),
            pltpu.VMEM((2, 4, 64, 1024), BF16),
            pltpu.SemaphoreType.DMA((8,)),
            pltpu.SemaphoreType.DMA((3,)),
            pltpu.SemaphoreType.DMA((3,)),
        ],
        compiler_params=pltpu.CompilerParams(
            collective_id=0, has_side_effects=True, vmem_limit_bytes=52 * 1024 * 1024
        ),
        cost_estimate=pl.CostEstimate(flops=6 * 10**9, bytes_accessed=11 * 10**6, transcendentals=2**19),
        name="airflow_block",
    )(tokens.reshape(192, D), ln_gain.reshape(1, D), w_qkv, w_out, w_rec, solid_top)


def solution(mesh):
    in_specs = (P("row", "aisle", None, None), P(), P(), P(), P(), P("row", "aisle"))
    out_specs = P(None, None, "row", "aisle")
    return jax.shard_map(body, mesh=mesh, in_specs=in_specs, out_specs=out_specs, check_vma=False)
```

time: 206 us -> 53.6 us (0.26)
  the two profiles are of different devices: /device:TPU:217 before, /device:TPU:2 now
where the time goes in v1:
time: 53.6 us; the launch traced here: 53.4 us
  Pallas kernels  49.1 us (92%)
  local copies, waits for them, and re-layouts  4.28 us (8%)
    pallas_call x1, Pallas kernels, body(): pl.pallas_call(kernel, out_shape=jax.ShapeDtypeStruct((4, 32, 24, 128), B...  49.1 us
    unnamed x7, local copies, waits for them, and re-layouts  3.31 us

profile of v1, /device:TPU:2, one launch (start us, length us, event | category | flops | bytes accessed | tf_op | source)
XLA Modules:
  0.0 53.4 jit_solution(17420623634089616062)
XLA Ops:
  0.0 1.0 %reshape.6.tokens_ref = bf16[192,512]{1,0:T(8,128)(2,1)S(1)} reshape(bf16[3,16,4,512]{3,2,1,0:T(4,128)(2,1)} %param.6) | data formatting | bytes 393216 | tf_op jit(solution)/shard_map/reshape | solution.py:356
  1.0 0.0 copy-start
  1.0 1.0 %copy-done = bf16[512,512]{1,0:T(8,128)(2,1)S(1)} copy-done((bf16[512,512]{1,0:T(8,128)(2,1)S(1)}, bf16[512,512]{1,0:T(8,128)(2,1)}, u32[]{:S(2)}) %copy-start) | copy-done | bytes 524312
  2.0 0.0 copy-start.1
  2.0 0.7 %copy-done.1 = s32[24,128]{1,0:T(8,128)S(1)} copy-done((s32[24,128]{1,0:T(8,128)S(1)}, s32[24,128]{1,0:T(8,128)}, u32[]{:S(2)}) %copy-start.1) | copy-done | bytes 12312
  2.7 0.0 copy-start.2
  2.7 0.7 %copy-done.2 = f32[512]{0:T(512)S(1)} copy-done((f32[512]{0:T(512)S(1)}, f32[512]{0:T(512)}, u32[]{:S(2)}) %copy-start.2) | copy-done | bytes 2072
  3.4 49.1 %airflow_block.1 = bf16[4,32,24,128]{3,2,1,0:T(8,128)(2,1)S(1)} custom-call(bf16[192,512]{1,0:T(8,128)(2,1)S(1)} %reshape.6.tokens_ref, f32[1,512]{1,0:T(1,128)S(1)} %bitcast.1, bf16[512,1536]{1,0:T(8,128)(2,1)} %w_qkv_hbm.1, bf16[512,512]{1,0:T(8,128)(2,1)S(1)} %copy-done, bf16[512,6912]{1,0:T(8,128)(2,1)} %w_rec_hbm.1, s32[24,128]{1,0:T(8,128)S(1)} %copy-done.1), custom_call_target="tpu_custom_call" | custom-call | flops 6000000000 | bytes 11000000 | tf_op jit(solution)/shard_map/airflow_block/pallas_call | solution.py:321
  52.5 0.9 %copy.8 = bf16[4,32,24,128]{3,2,1,0:T(8,128)(2,1)} copy(bf16[4,32,24,128]{3,2,1,0:T(8,128)(2,1)S(1)} %airflow_block.1) | data formatting | bytes 1572864
Async XLA Ops:
  1.0 1.0 %copy-start = (bf16[512,512]{1,0:T(8,128)(2,1)S(1)}, bf16[512,512]{1,0:T(8,128)(2,1)}, u32[]{:S(2)}) copy-start(bf16[512,512]{1,0:T(8,128)(2,1)} %w_out_hbm.1) | copy-start | bytes 1572868
  2.0 0.7 %copy-start.1 = (s32[24,128]{1,0:T(8,128)S(1)}, s32[24,128]{1,0:T(8,128)}, u32[]{:S(2)}) copy-start(s32[24,128]{1,0:T(8,128)} %solid_ref.1) | copy-start | bytes 36868
  2.7 0.7 %copy-start.2 = (f32[512]{0:T(512)S(1)}, f32[512]{0:T(512)}, u32[]{:S(2)}) copy-start(f32[512]{0:T(512)} %param.7) | copy-start | bytes 6148

commit v2 on v1

--- a/solution.py
+++ b/solution.py
@@ -133,17 +133,23 @@
 
 
 def kernel(
-    tokens_ref, gain_ref, w_qkv_hbm, w_out_hbm, w_rec_hbm, solid_ref,
+    tokens_hbm, gain_hbm, w_qkv_hbm, w_out_hbm, w_rec_hbm, solid_hbm,
     out_ref,
-    w_qkv, w_out, w_rec, send1, recv1, send2, cat, row_halo,
+    tokens, gain, solid_ref, w_qkv, w_out, w_rec, send1, recv1, send2, cat, row_halo,
     w_sel, main_w, side_w, edge_w, halo_sel, perm, edge_sel, row_sel,
     shifted, acc, edge_acc, ready,
-    load_sem, send_sem, recv_sem,
+    load_sem, send_sem, recv_sem, halo_send_sem, halo_recv_sem,
 ):
     i, k = lax.axis_index("row"), lax.axis_index("aisle")
 
-    loads = [pltpu.make_async_copy(w_qkv_hbm, w_qkv, load_sem.at[6]),
-             pltpu.make_async_copy(w_out_hbm, w_out, load_sem.at[7])]
+    token_load = pltpu.make_async_copy(tokens_hbm, tokens, load_sem.at[6])
+    token_load.start()
+    loads = [
+        pltpu.make_async_copy(gain_hbm, gain, load_sem.at[7]),
+        pltpu.make_async_copy(w_qkv_hbm, w_qkv, load_sem.at[8]),
+        pltpu.make_async_copy(w_out_hbm, w_out, load_sem.at[9]),
+        pltpu.make_async_copy(solid_hbm, solid_ref, load_sem.at[10]),
+    ]
     for load in loads:
         load.start()
 
@@ -155,19 +161,30 @@
         rec_load(q).start()
 
     barrier = pltpu.get_barrier_semaphore()
+    up, down, right, left = i + 1, i - 1, k + 1, k - 1
+    has_up, has_down, has_right, has_left = i < N_ROW - 1, i > 0, k < N_AISLE - 1, k > 0
+    neighbours = [
+        ((i, right), has_right), ((i, left), has_left),
+        ((up, right), has_up & has_right), ((up, left), has_up & has_left),
+        ((down, right), has_down & has_right), ((down, left), has_down & has_left),
+    ]
 
     @pl.loop(1, N_ROW)
     def _(step):
         pl.semaphore_signal(barrier, inc=1, device_id=(lax.rem(i + step, N_ROW), k), device_id_type=MESH)
 
-    up, down = lax.rem(i + 1, N_ROW), lax.rem(i + N_ROW - 1, N_ROW)
-    right, left = lax.rem(k + 1, N_AISLE), lax.rem(k + N_AISLE - 1, N_AISLE)
-    for device in ((i, right), (i, left), (up, right), (up, left), (down, right), (down, left)):
-        pl.semaphore_signal(barrier, inc=1, device_id=device, device_id_type=MESH)
-
-    send1[...] = dot(send_selector(), tokens_ref[...]).reshape(32, 8, D).astype(BF16)
+    for device, present in neighbours:
+        @pl.when(present)
+        def _():
+            pl.semaphore_signal(barrier, inc=1, device_id=device, device_id_type=MESH)
+
+    token_load.wait()
+    mine = tokens[...].astype(F32).reshape(192, D).astype(BF16)
+    send1[...] = dot(send_selector(), mine).reshape(32, 8, D).astype(BF16)
     recv1[i] = send1[i]
-    pl.semaphore_wait(barrier, N_ROW - 1 + 6)
+    across = has_left.astype(I32) + has_right.astype(I32)
+    along = has_down.astype(I32) + has_up.astype(I32)
+    pl.semaphore_wait(barrier, N_ROW - 1 + across * (1 + along))
 
     def exchange(source, target, sem):
         @pl.loop(1, N_ROW)
@@ -183,7 +200,7 @@
         return pltpu.make_async_remote_copy(
             src_ref=source.at[pl.ds(start, count)], dst_ref=target.at[pl.ds(start, count)],
             send_sem=send_sem.at[sem], recv_sem=recv_sem.at[sem],
-            device_id=(up, k), device_id_type=MESH,
+            device_id=(lax.rem(i + 1, N_ROW), k), device_id_type=MESH,
         )
 
     exchange(send1, recv1, 0)
@@ -221,7 +238,7 @@
     drain(send1, recv1, N_ROW - 1, 0).wait_recv()
 
     x = recv1[...].astype(F32).reshape(256, D)
-    block_out = attend_lines(x, gain_ref[...], w_qkv[...], w_out[...])
+    block_out = attend_lines(x, gain[...], w_qkv[...], w_out[...])
     send2[...] = block_out.reshape(32, 8, D).astype(BF16)
     cat[i] = send2[i]
     exchange(send2, cat, 1)
@@ -233,6 +250,15 @@
         halo_sel[n] = halo_selector(da, i, k)
     shifted[0] = jnp.zeros(shifted.shape[1:], BF16)
     shifted[5] = jnp.zeros(shifted.shape[1:], BF16)
+    for n, size, present in ((32, 8, has_down), (40, 8, has_up)):
+        @pl.when(jnp.logical_not(present))
+        def _():
+            cat[n : n + size] = jnp.zeros((size, 8, D), BF16)
+    sides = [has_left, has_right, has_down & has_left, has_down & has_right, has_up & has_left, has_up & has_right]
+    for n, present in enumerate(sides):
+        @pl.when(jnp.logical_not(present))
+        def _():
+            cat[48 + 2 * n : 50 + 2 * n] = jnp.zeros((2, 8, D), BF16)
     cat[60:64] = jnp.zeros((4, 8, D), BF16)
 
     @pl.loop(3, 6)
@@ -245,25 +271,42 @@
     own = cat[:32].astype(F32).reshape(256, D).astype(BF16)
     row_halo[...] = dot(row_sel[...], own).reshape(16, 8, D).astype(BF16)
 
-    def halo_copy(source, at, size, device):
-        pltpu.make_async_remote_copy(
-            src_ref=source, dst_ref=cat.at[pl.ds(at, size)],
-            send_sem=send_sem.at[2], recv_sem=recv_sem.at[2],
+    lowest, highest = cat.at[pl.ds(0, 2)], cat.at[pl.ds(30, 2)]
+    halos = [
+        (row_halo.at[pl.ds(0, 8)], 40, (down, k), has_down),
+        (row_halo.at[pl.ds(8, 8)], 32, (up, k), has_up),
+        (lowest, 50, (i, left), has_left),
+        (highest, 48, (i, right), has_right),
+        (highest, 52, (up, right), has_up & has_right),
+        (lowest, 54, (up, left), has_up & has_left),
+        (highest, 56, (down, right), has_down & has_right),
+        (lowest, 58, (down, left), has_down & has_left),
+    ]
+
+    def halo_copy(n):
+        source, at, device, _ = halos[n]
+        return pltpu.make_async_remote_copy(
+            src_ref=source, dst_ref=cat.at[pl.ds(at, 8 if n < 2 else 2)],
+            send_sem=halo_send_sem.at[n], recv_sem=halo_recv_sem.at[n],
             device_id=device, device_id_type=MESH,
-        ).start()
-
-    lowest, highest = cat.at[pl.ds(0, 2)], cat.at[pl.ds(30, 2)]
-    halo_copy(row_halo.at[pl.ds(0, 8)], 40, 8, (down, k))
-    halo_copy(row_halo.at[pl.ds(8, 8)], 32, 8, (up, k))
-    halo_copy(lowest, 50, 2, (i, left))
-    halo_copy(highest, 48, 2, (i, right))
-    halo_copy(highest, 52, 2, (up, right))
-    halo_copy(lowest, 54, 2, (up, left))
-    halo_copy(highest, 56, 2, (down, right))
-    halo_copy(lowest, 58, 2, (down, left))
+        )
+
+    for n in range(8):
+        @pl.when(halos[n][3])
+        def _():
+            halo_copy(n).start()
+
     drain(send2, cat, N_ROW - 1, 1).wait_send()
-    drain(cat, cat, 28, 2, 32).wait_recv()
-    drain(cat, cat, 28, 2, 32).wait_send()
+    arrives = [has_up, has_down, has_right, has_left, has_down & has_left, has_down & has_right, has_up & has_left, has_up & has_right]
+    for n in range(8):
+        @pl.when(arrives[n])
+        def _():
+            halo_copy(n).wait_recv()
+
+        @pl.when(halos[n][3])
+        def _():
+            halo_copy(n).wait_send()
+
 
     gathered = cat[...].astype(F32).reshape(512, D).astype(BF16)
     for n in range(3):
@@ -272,58 +315,61 @@
 
     spans = ((0, 0, 8, 2), (-1, 0, 2, 10), (1, 6, 2, 0))
 
-    @pl.loop(0, 4)
-    def _(c):
-        for dz, z, n, kz in spans:
-            pairs = pl.ds(kz // 2, n // 2)
-            here = pl.ds(1 + dz, 4)
-            level = pl.ds(z, n)
-            for part in range(3):
-                token_part = shifted[here, 1:5, :, part * D : (part + 1) * D].reshape(256, D)
-                if part == 0:
-                    rows, size, y = main_w[c, :, pairs], 8, 0
-                else:
-                    rows, size, y = side_w[part - 1, c, :, pairs], 2, 6 * (part - 1)
-                found = dot_nt(rows.reshape(-1, D), token_part).reshape(size, n, 8, 256)
-                if dz == 0 and part == 0:
-                    acc[c] = found
-                else:
-                    acc[c, pl.ds(y, size), level] += found
-            for side in range(2):
-                token_part = shifted[here, pl.ds(2 * side, 4)].reshape(256, 3 * D)
-                rows = edge_w[side, c, pl.ds(kz, n)].reshape(-1, 3 * D)
-                found = dot_nt(rows, token_part).reshape(n, 16, 256)
-                if dz == 0:
-                    edge_acc[c, :, side] = found
-                else:
-                    edge_acc[c, level, side] += found
+    for dz, z, n, kz in spans:
+        pairs = pl.ds(kz // 2, n // 2)
+        here = pl.ds(1 + dz, 4)
+        level = pl.ds(z, n)
+        for part in range(3):
+            token_part = shifted[here, 1:5, :, part * D : (part + 1) * D].reshape(256, D)
+            if part == 0:
+                rows, size, y = main_w[:, :, pairs], 8, 0
+            else:
+                rows, size, y = side_w[part - 1, :, :, pairs], 2, 6 * (part - 1)
+            found = dot_nt(rows.reshape(-1, D), token_part).reshape(4, size, n, 8, 256)
+            if dz == 0 and part == 0:
+                acc[...] = found
+            else:
+                acc[:, pl.ds(y, size), level] += found
+        for side in range(2):
+            token_part = shifted[here, pl.ds(2 * side, 4)].reshape(256, 3 * D)
+            rows = edge_w[side, :, pl.ds(kz, n)].reshape(-1, 3 * D)
+            found = dot_nt(rows, token_part).reshape(4, n, 16, 256)
+            if dz == 0:
+                edge_acc[:, :, side] = found
+            else:
+                edge_acc[:, level, side] += found
+    for c in range(4):
         edges = edge_acc[c].reshape(256, 256).astype(BF16)
         total = acc[c].reshape(512, 256) + dot(edge_sel[...], edges)
         total = total.astype(BF16)
         for y in range(8):
             for b in range(2):
                 ready[b, c, :, y * 128 : (y + 1) * 128] = total[y * 64 : (y + 1) * 64, b * 128 : (b + 1) * 128]
-
     solid = solid_ref[...]
-    for h in range(4):
-        b, low = h // 2, h % 2
-        cells = dot(ready[b].reshape(256, 1024), perm[:, low * 384 : (low + 1) * 384])
-        cells = jnp.concatenate(
-            [cells[:, r * 128 : (r + 1) * 128].reshape(4, 8, 8, 128) for r in range(3)], axis=2
-        )
-        level = iota((4, 8, 24, 128), 1) + 8 * h
-        out_ref[:, 8 * h : 8 * h + 8] = jnp.where(level < solid[None, None], 0.0, cells).astype(BF16)
+    for low in range(2):
+        cells = dot(ready[...].reshape(512, 1024), perm[:, low * 384 : (low + 1) * 384])
+        for b in range(2):
+            h = 2 * b + low
+            part = cells[b * 256 : (b + 1) * 256]
+            part = jnp.concatenate(
+                [part[:, r * 128 : (r + 1) * 128].reshape(4, 8, 8, 128) for r in range(3)], axis=2
+            )
+            level = iota((4, 8, 24, 128), 1) + 8 * h
+            out_ref[:, 8 * h : 8 * h + 8] = jnp.where(level < solid[None, None], 0.0, part).astype(BF16)
 
 
 def body(tokens, ln_gain, w_qkv, w_out, w_rec, solid_top):
     vmem = pl.BlockSpec(memory_space=pltpu.VMEM)
-    hbm = pl.BlockSpec(memory_space=pl.ANY)
+    hbm = pl.BlockSpec(memory_space=pltpu.HBM)
     return pl.pallas_call(
         kernel,
         out_shape=jax.ShapeDtypeStruct((4, 32, 24, 128), BF16),
-        in_specs=[vmem, vmem, hbm, hbm, hbm, vmem],
+        in_specs=[hbm] * 6,
         out_specs=vmem,
         scratch_shapes=[
+            pltpu.VMEM((3, 16, 4, D), BF16),
+            pltpu.VMEM((1, D), F32),
+            pltpu.VMEM((24, 128), I32),
             pltpu.VMEM((D, 3 * D), BF16),
             pltpu.VMEM((D, D), BF16),
             pltpu.VMEM((D, 6912), BF16),
@@ -344,16 +390,18 @@
             pltpu.VMEM((4, 8, 8, 8, 256), F32),
             pltpu.VMEM((4, 8, 2, 16, 256), F32),
             pltpu.VMEM((2, 4, 64, 1024), BF16),
+            pltpu.SemaphoreType.DMA((11,)),
+            pltpu.SemaphoreType.DMA((2,)),
+            pltpu.SemaphoreType.DMA((2,)),
             pltpu.SemaphoreType.DMA((8,)),
-            pltpu.SemaphoreType.DMA((3,)),
-            pltpu.SemaphoreType.DMA((3,)),
+            pltpu.SemaphoreType.DMA((8,)),
         ],
         compiler_params=pltpu.CompilerParams(
-            collective_id=0, has_side_effects=True, vmem_limit_bytes=52 * 1024 * 1024
+            collective_id=0, has_side_effects=True, vmem_limit_bytes=60 * 1024 * 1024
         ),
         cost_estimate=pl.CostEstimate(flops=6 * 10**9, bytes_accessed=11 * 10**6, transcendentals=2**19),
         name="airflow_block",
-    )(tokens.reshape(192, D), ln_gain.reshape(1, D), w_qkv, w_out, w_rec, solid_top)
+    )(tokens, ln_gain.reshape(1, D), w_qkv, w_out, w_rec, solid_top)
 
 
 def solution(mesh):

time: 53.6 us -> 41.5 us (0.77)
  the two profiles are of different devices: /device:TPU:2 before, /device:TPU:7 now
where the time goes in v2:
time: 41.5 us; the launch traced here: 41 us
  Pallas kernels  38.9 us (94%)
  local copies, waits for them, and re-layouts  2.09 us (5%)
    pallas_call x1, Pallas kernels, body(): pl.pallas_call(kernel, out_shape=jax.ShapeDtypeStruct((4, 32, 24, 128), B...  38.9 us
    unnamed x1, local copies, waits for them, and re-layouts  2.09 us

profile of v2, /device:TPU:7, one launch (start us, length us, event | category | flops | bytes accessed | tf_op | source)
XLA Modules:
  0.0 41.0 jit_solution(6974614452086026004)
XLA Ops:
  0.0 38.9 %airflow_block.1 = bf16[4,32,24,128]{3,2,1,0:T(8,128)(2,1)} custom-call(bf16[3,16,4,512]{3,2,1,0:T(4,128)(2,1)} %tokens_hbm.1, f32[1,512]{1,0:T(1,128)} %bitcast.1, bf16[512,1536]{1,0:T(8,128)(2,1)} %w_qkv_hbm.1, bf16[512,512]{1,0:T(8,128)(2,1)} %w_out_hbm.1, bf16[512,6912]{1,0:T(8,128)(2,1)} %w_rec_hbm.1, s32[24,128]{1,0:T(8,128)} %solid_hbm.1), custom_call_target="tpu_custom_call" | custom-call | flops 6000000000 | bytes 11000000 | tf_op jit(solution)/shard_map/airflow_block/pallas_call | solution.py:364
  38.9 2.1 %copy.8 = bf16[4,32,24,128]{3,2,1,0:T(8,128)(2,1)} copy(bf16[4,32,24,128]{3,2,1,0:T(8,128)(2,1)} %airflow_block.1) | data formatting | bytes 1572864

commit v3 on v2

--- a/solution.py
+++ b/solution.py
@@ -68,8 +68,8 @@
     inside = jnp.where(
         r < 0, 256 + a * 4 + h, jnp.where(r > 2, 320 + a * 4 + h, a * 16 + h * 4 + r)
     )
-    left = jnp.where(r < 0, 416 + h * 4 + 2, jnp.where(r > 2, 448 + h * 4, 384 + h * 4 + r))
-    right = jnp.where(r < 0, 432 + h * 4 + 2, jnp.where(r > 2, 464 + h * 4, 400 + h * 4 + r))
+    left = jnp.where(r < 0, 416 + h, jnp.where(r > 2, 432 + h, 384 + h * 4 + r))
+    right = jnp.where(r < 0, 424 + h, jnp.where(r > 2, 440 + h, 400 + h * 4 + r))
     source = jnp.where(a < 0, left, jnp.where(a > 15, right, inside))
     absent = (
         (r > 3)
@@ -99,9 +99,12 @@
 
 
 def row_halo_selector():
-    row = iota((128, 1), 0)
-    source = (row & 63) * 4 + jnp.where(row >= 64, 2, 0)
-    return one_hot(iota((128, 256), 1) == source)
+    row = iota((160, 1), 0)
+    edge = (row & 63) * 4 + jnp.where(row >= 64, 2, 0)
+    block = (row - 128) >> 3
+    corner = (row & 7) * 4 + jnp.where(block < 2, 2, 0) + jnp.where((block & 1) == 0, 240, 0)
+    source = jnp.where(row < 128, edge, jnp.where((row & 7) < 4, corner, -1))
+    return one_hot(iota((160, 256), 1) == source)
 
 
 def attend_lines(x, gain, w_qkv, w_out):
@@ -133,12 +136,12 @@
 
 
 def kernel(
-    tokens_hbm, gain_hbm, w_qkv_hbm, w_out_hbm, w_rec_hbm, solid_hbm,
+    tokens_hbm, gain_hbm, w_qkv_hbm, w_out_hbm, w_rec_hbm,
     out_ref,
-    tokens, gain, solid_ref, w_qkv, w_out, w_rec, send1, recv1, send2, cat, row_halo,
+    tokens, gain, w_qkv, w_out, w_rec, send1, recv1, send2, cat, row_halo,
     w_sel, main_w, side_w, edge_w, halo_sel, perm, edge_sel, row_sel,
-    shifted, acc, edge_acc, ready,
-    load_sem, send_sem, recv_sem, halo_send_sem, halo_recv_sem,
+    shifted, acc, edge_acc, ready, found_cells,
+    load_sem, send_sem, recv_sem, halo_send_sem, halo_recv_sem, store_sem,
 ):
     i, k = lax.axis_index("row"), lax.axis_index("aisle")
 
@@ -148,7 +151,6 @@
         pltpu.make_async_copy(gain_hbm, gain, load_sem.at[7]),
         pltpu.make_async_copy(w_qkv_hbm, w_qkv, load_sem.at[8]),
         pltpu.make_async_copy(w_out_hbm, w_out, load_sem.at[9]),
-        pltpu.make_async_copy(solid_hbm, solid_ref, load_sem.at[10]),
     ]
     for load in loads:
         load.start()
@@ -258,8 +260,9 @@
     for n, present in enumerate(sides):
         @pl.when(jnp.logical_not(present))
         def _():
-            cat[48 + 2 * n : 50 + 2 * n] = jnp.zeros((2, 8, D), BF16)
-    cat[60:64] = jnp.zeros((4, 8, D), BF16)
+            at, size = (48 + 2 * n, 2) if n < 2 else (50 + n, 1)
+            cat[at : at + size] = jnp.zeros((size, 8, D), BF16)
+    cat[56:64] = jnp.zeros((8, 8, D), BF16)
 
     @pl.loop(3, 6)
     def _(q):
@@ -268,33 +271,47 @@
     drain(send1, recv1, N_ROW - 1, 0).wait_send()
     drain(send2, cat, N_ROW - 1, 1).wait_recv()
 
-    own = cat[:32].astype(F32).reshape(256, D).astype(BF16)
-    row_halo[...] = dot(row_sel[...], own).reshape(16, 8, D).astype(BF16)
-
     lowest, highest = cat.at[pl.ds(0, 2)], cat.at[pl.ds(30, 2)]
     halos = [
-        (row_halo.at[pl.ds(0, 8)], 40, (down, k), has_down),
-        (row_halo.at[pl.ds(8, 8)], 32, (up, k), has_up),
-        (lowest, 50, (i, left), has_left),
-        (highest, 48, (i, right), has_right),
-        (highest, 52, (up, right), has_up & has_right),
-        (lowest, 54, (up, left), has_up & has_left),
-        (highest, 56, (down, right), has_down & has_right),
-        (lowest, 58, (down, left), has_down & has_left),
+        (row_halo.at[pl.ds(0, 8)], 40, 8, (down, k), has_down),
+        (row_halo.at[pl.ds(8, 8)], 32, 8, (up, k), has_up),
+        (lowest, 50, 2, (i, left), has_left),
+        (highest, 48, 2, (i, right), has_right),
+        (row_halo.at[pl.ds(16, 1)], 52, 1, (up, right), has_up & has_right),
+        (row_halo.at[pl.ds(17, 1)], 53, 1, (up, left), has_up & has_left),
+        (row_halo.at[pl.ds(18, 1)], 54, 1, (down, right), has_down & has_right),
+        (row_halo.at[pl.ds(19, 1)], 55, 1, (down, left), has_down & has_left),
     ]
 
     def halo_copy(n):
-        source, at, device, _ = halos[n]
+        source, at, size, device, _ = halos[n]
         return pltpu.make_async_remote_copy(
-            src_ref=source, dst_ref=cat.at[pl.ds(at, 8 if n < 2 else 2)],
+            src_ref=source, dst_ref=cat.at[pl.ds(at, size)],
             send_sem=halo_send_sem.at[n], recv_sem=halo_recv_sem.at[n],
             device_id=device, device_id_type=MESH,
         )
 
-    for n in range(8):
-        @pl.when(halos[n][3])
-        def _():
-            halo_copy(n).start()
+    def start_halos(numbers):
+        for n in numbers:
+            @pl.when(halos[n][4])
+            def _():
+                halo_copy(n).start()
+
+    start_halos((2, 3))
+    own = cat[:32].astype(F32).reshape(256, D).astype(BF16)
+    row_halo[...] = dot(row_sel[...], own).reshape(20, 8, D).astype(BF16)
+    start_halos((4, 5, 6, 7, 0, 1))
+
+    shifted[1:5, :, :, :D] = dot(halo_sel[0, :, :256], own).reshape(4, 6, 16, D).astype(BF16)
+    spans = ((0, 0, 8, 2), (-1, 0, 2, 10), (1, 6, 2, 0))
+    for dz, z, n, kz in spans:
+        token_part = shifted[1 + dz : 5 + dz, 1:5, :, :D].reshape(256, D)
+        rows = main_w[:, :, kz // 2 : (kz + n) // 2].reshape(-1, D)
+        found = dot_nt(rows, token_part).reshape(4, 8, n, 8, 256)
+        if dz == 0:
+            acc[...] = found
+        else:
+            acc[:, :, z : z + n] += found
 
     drain(send2, cat, N_ROW - 1, 1).wait_send()
     arrives = [has_up, has_down, has_right, has_left, has_down & has_left, has_down & has_right, has_up & has_left, has_up & has_right]
@@ -303,7 +320,7 @@
         def _():
             halo_copy(n).wait_recv()
 
-        @pl.when(halos[n][3])
+        @pl.when(halos[n][4])
         def _():
             halo_copy(n).wait_send()
 
@@ -316,21 +333,12 @@
     spans = ((0, 0, 8, 2), (-1, 0, 2, 10), (1, 6, 2, 0))
 
     for dz, z, n, kz in spans:
-        pairs = pl.ds(kz // 2, n // 2)
         here = pl.ds(1 + dz, 4)
         level = pl.ds(z, n)
-        for part in range(3):
-            token_part = shifted[here, 1:5, :, part * D : (part + 1) * D].reshape(256, D)
-            if part == 0:
-                rows, size, y = main_w[:, :, pairs], 8, 0
-            else:
-                rows, size, y = side_w[part - 1, :, :, pairs], 2, 6 * (part - 1)
-            found = dot_nt(rows.reshape(-1, D), token_part).reshape(4, size, n, 8, 256)
-            if dz == 0 and part == 0:
-                acc[...] = found
-            else:
-                acc[:, pl.ds(y, size), level] += found
         for side in range(2):
+            token_part = shifted[here, 1:5, :, (side + 1) * D : (side + 2) * D].reshape(256, D)
+            rows = side_w[side, :, :, pl.ds(kz // 2, n // 2)].reshape(-1, D)
+            acc[:, pl.ds(6 * side, 2), level] += dot_nt(rows, token_part).reshape(4, 2, n, 8, 256)
             token_part = shifted[here, pl.ds(2 * side, 4)].reshape(256, 3 * D)
             rows = edge_w[side, :, pl.ds(kz, n)].reshape(-1, 3 * D)
             found = dot_nt(rows, token_part).reshape(4, n, 16, 256)
@@ -345,31 +353,33 @@
         for y in range(8):
             for b in range(2):
                 ready[b, c, :, y * 128 : (y + 1) * 128] = total[y * 64 : (y + 1) * 64, b * 128 : (b + 1) * 128]
-    solid = solid_ref[...]
+    stores = []
     for low in range(2):
         cells = dot(ready[...].reshape(512, 1024), perm[:, low * 384 : (low + 1) * 384])
         for b in range(2):
             h = 2 * b + low
-            part = cells[b * 256 : (b + 1) * 256]
-            part = jnp.concatenate(
-                [part[:, r * 128 : (r + 1) * 128].reshape(4, 8, 8, 128) for r in range(3)], axis=2
+            for r in range(3):
+                part = cells[b * 256 : (b + 1) * 256, r * 128 : (r + 1) * 128]
+                found_cells[h, :, :, 8 * r : 8 * r + 8] = part.reshape(4, 8, 8, 128)
+            store = pltpu.make_async_copy(
+                found_cells.at[h], out_ref.at[:, pl.ds(8 * h, 8)], store_sem.at[h]
             )
-            level = iota((4, 8, 24, 128), 1) + 8 * h
-            out_ref[:, 8 * h : 8 * h + 8] = jnp.where(level < solid[None, None], 0.0, part).astype(BF16)
+            store.start()
+            stores.append(store)
+    for store in stores:
+        store.wait()
 
 
 def body(tokens, ln_gain, w_qkv, w_out, w_rec, solid_top):
-    vmem = pl.BlockSpec(memory_space=pltpu.VMEM)
     hbm = pl.BlockSpec(memory_space=pltpu.HBM)
-    return pl.pallas_call(
+    cells = pl.pallas_call(
         kernel,
-        out_shape=jax.ShapeDtypeStruct((4, 32, 24, 128), BF16),
-        in_specs=[hbm] * 6,
-        out_specs=vmem,
+        out_shape=jax.ShapeDtypeStruct((4, 32, 24, 128), F32),
+        in_specs=[hbm] * 5,
+        out_specs=hbm,
         scratch_shapes=[
             pltpu.VMEM((3, 16, 4, D), BF16),
             pltpu.VMEM((1, D), F32),
-            pltpu.VMEM((24, 128), I32),
             pltpu.VMEM((D, 3 * D), BF16),
             pltpu.VMEM((D, D), BF16),
             pltpu.VMEM((D, 6912), BF16),
@@ -377,7 +387,7 @@
             pltpu.VMEM((32, 8, D), BF16),
             pltpu.VMEM((32, 8, D), BF16),
             pltpu.VMEM((64, 8, D), BF16),
-            pltpu.VMEM((16, 8, D), BF16),
+            pltpu.VMEM((20, 8, D), BF16),
             pltpu.VMEM((8, 192, 256), BF16),
             pltpu.VMEM((4, 8, 6, 16, D), BF16),
             pltpu.VMEM((2, 4, 2, 6, 16, D), BF16),
@@ -385,23 +395,27 @@
             pltpu.VMEM((3, 384, 512), BF16),
             pltpu.VMEM((1024, 768), BF16),
             pltpu.VMEM((512, 256), BF16),
-            pltpu.VMEM((128, 256), BF16),
+            pltpu.VMEM((160, 256), BF16),
             pltpu.VMEM((6, 6, 16, 3 * D), BF16),
             pltpu.VMEM((4, 8, 8, 8, 256), F32),
             pltpu.VMEM((4, 8, 2, 16, 256), F32),
             pltpu.VMEM((2, 4, 64, 1024), BF16),
-            pltpu.SemaphoreType.DMA((11,)),
+            pltpu.VMEM((4, 4, 8, 24, 128), F32),
+            pltpu.SemaphoreType.DMA((10,)),
             pltpu.SemaphoreType.DMA((2,)),
             pltpu.SemaphoreType.DMA((2,)),
             pltpu.SemaphoreType.DMA((8,)),
             pltpu.SemaphoreType.DMA((8,)),
+            pltpu.SemaphoreType.DMA((4,)),
         ],
         compiler_params=pltpu.CompilerParams(
             collective_id=0, has_side_effects=True, vmem_limit_bytes=60 * 1024 * 1024
         ),
         cost_estimate=pl.CostEstimate(flops=6 * 10**9, bytes_accessed=11 * 10**6, transcendentals=2**19),
         name="airflow_block",
-    )(tokens, ln_gain.reshape(1, D), w_qkv, w_out, w_rec, solid_top)
+    )(tokens, ln_gain.reshape(1, D), w_qkv, w_out, w_rec)
+    level = iota((4, 32, 24, 128), 1)
+    return jnp.where(level < solid_top[None, None], 0.0, cells).astype(BF16)
 
 
 def solution(mesh):

time: 41.5 us -> 42.5 us (1.024)
  other arithmetic: 0 us -> 2.44 us
  local copies, waits for them, and re-layouts: 2.09 us -> 0.01 us
  Pallas kernels: 38.9 us -> 39.5 us
    convert_element_type x0 -> x1, other arithmetic: none -> 2.44 us  [body(): return jnp.where(level < solid_top[None, None], 0.0, cells).astype(BF16)]
    unnamed x1 -> x2, local copies, waits for them, and re-layouts: 2.09 us -> 0.01 us
    pallas_call x1, Pallas kernels: 38.9 us -> 39.5 us  [body(): pl.pallas_call(kernel, out_shape=jax.ShapeDtypeStruct((4, 32, 24, 128), F...]
where the time goes in v3:
time: 42.5 us; the launch traced here: 42 us
  Pallas kernels  39.5 us (93%)
  other arithmetic  2.44 us (6%)
    pallas_call x1, Pallas kernels, body(): pl.pallas_call(kernel, out_shape=jax.ShapeDtypeStruct((4, 32, 24, 128), F...  39.5 us
    convert_element_type x1, other arithmetic, body(): return jnp.where(level < solid_top[None, None], 0.0, cells).astype(BF16)  2.44 us

profile of v3, /device:TPU:7, one launch (start us, length us, event | category | flops | bytes accessed | tf_op | source)
XLA Modules:
  0.0 42.0 jit_solution(2146842279995121744)
XLA Ops:
  0.0 0.0 copy-start
  0.0 39.5 %airflow_block.1 = f32[4,32,24,128]{3,2,1,0:T(8,128)} custom-call(bf16[3,16,4,512]{3,2,1,0:T(4,128)(2,1)} %tokens_hbm.1, f32[1,512]{1,0:T(1,128)} %bitcast.1, bf16[512,1536]{1,0:T(8,128)(2,1)} %w_qkv_hbm.1, bf16[512,512]{1,0:T(8,128)(2,1)} %w_out_hbm.1, bf16[512,6912]{1,0:T(8,128)(2,1)} %w_rec_hbm.1), custom_call_target="tpu_custom_call" | custom-call | flops 6000000000 | bytes 11000000 | tf_op jit(solution)/shard_map/airflow_block/pallas_call | solution.py:375
  39.5 0.0 copy-done
  39.5 2.4 %select_convert_fusion = bf16[4,32,24,128]{3,2,1,0:T(8,128)(2,1)} fusion(f32[4,32,24,128]{3,2,1,0:T(8,128)} %airflow_block.1, s32[24,128]{1,0:T(8,128)S(1)} %copy-done), kind=kLoop, calls=%fused_computation | loop fusion | flops 786432 | bytes 2371584 | tf_op jit(solution)/shard_map/convert_element_type | solution.py:418
Async XLA Ops:
  0.0 39.5 %copy-start = (s32[24,128]{1,0:T(8,128)S(1)}, s32[24,128]{1,0:T(8,128)}, u32[]{:S(2)}) copy-start(s32[24,128]{1,0:T(8,128)} %param.11) | copy-start | bytes 36868

commit v4 on v2

--- a/solution.py
+++ b/solution.py
@@ -59,27 +59,20 @@
     return one_hot(iota((192, 256), 1) - 16 * step == column)
 
 
-def halo_selector(da, row_index, aisle_index):
-    q = iota((384, 1), 0)
-    h = jnp.where(q >= 288, 3, jnp.where(q >= 192, 2, jnp.where(q >= 96, 1, 0)))
-    rest = q - 96 * h
-    r = (rest >> 4) - 1
-    a = (rest & 15) + da
-    inside = jnp.where(
-        r < 0, 256 + a * 4 + h, jnp.where(r > 2, 320 + a * 4 + h, a * 16 + h * 4 + r)
-    )
-    left = jnp.where(r < 0, 416 + h * 4 + 2, jnp.where(r > 2, 448 + h * 4, 384 + h * 4 + r))
-    right = jnp.where(r < 0, 432 + h * 4 + 2, jnp.where(r > 2, 464 + h * 4, 400 + h * 4 + r))
-    source = jnp.where(a < 0, left, jnp.where(a > 15, right, inside))
-    absent = (
-        (r > 3)
-        | ((r < 0) & (row_index == 0))
-        | ((r > 2) & (row_index == N_ROW - 1))
-        | ((a < 0) & (aisle_index == 0))
-        | ((a > 15) & (aisle_index == N_AISLE - 1))
-    )
-    source = jnp.where(absent, -1, source)
-    return one_hot(iota((384, 512), 1) == source)
+def near_selector(da):
+    q = iota((192, 1), 0)
+    h = jnp.where(q >= 144, 3, jnp.where(q >= 96, 2, jnp.where(q >= 48, 1, 0)))
+    rest = q - 48 * h
+    r, a = rest >> 4, (rest & 15) + da
+    block = jnp.where(a < 0, 16, jnp.where(a > 15, 17, a))
+    return one_hot(iota((192, 384), 1) == block * 16 + h * 4 + r)
+
+
+def far_selector(da):
+    q = iota((128, 1), 0)
+    h, side, a = q >> 5, (q >> 4) & 1, (q & 15) + da
+    block = jnp.where(a < 0, 16, jnp.where(a > 15, 17, a))
+    return one_hot(iota((128, 256), 1) == side * 72 + block * 4 + h)
 
 
 def lane_permutation():
@@ -99,9 +92,9 @@
 
 
 def row_halo_selector():
-    row = iota((128, 1), 0)
-    source = (row & 63) * 4 + jnp.where(row >= 64, 2, 0)
-    return one_hot(iota((128, 256), 1) == source)
+    row = iota((144, 1), 0)
+    source = jnp.where(row >= 72, (row - 72) * 4 + 2, row * 4)
+    return one_hot(iota((144, 384), 1) == source)
 
 
 def attend_lines(x, gain, w_qkv, w_out):
@@ -135,8 +128,8 @@
 def kernel(
     tokens_hbm, gain_hbm, w_qkv_hbm, w_out_hbm, w_rec_hbm, solid_hbm,
     out_ref,
-    tokens, gain, solid_ref, w_qkv, w_out, w_rec, send1, recv1, send2, cat, row_halo,
-    w_sel, main_w, side_w, edge_w, halo_sel, perm, edge_sel, row_sel,
+    tokens, gain, solid_ref, w_qkv, w_out, w_rec, send1, recv1, send2, near, far, row_halo,
+    w_sel, main_w, side_w, edge_w, near_sel, far_sel, perm, edge_sel, row_sel,
     shifted, acc, edge_acc, ready,
     load_sem, send_sem, recv_sem, halo_send_sem, halo_recv_sem,
 ):
@@ -161,30 +154,26 @@
         rec_load(q).start()
 
     barrier = pltpu.get_barrier_semaphore()
-    up, down, right, left = i + 1, i - 1, k + 1, k - 1
+    up, down = lax.rem(i + 1, N_ROW), lax.rem(i + N_ROW - 1, N_ROW)
+    right, left = lax.rem(k + 1, N_AISLE), lax.rem(k + N_AISLE - 1, N_AISLE)
     has_up, has_down, has_right, has_left = i < N_ROW - 1, i > 0, k < N_AISLE - 1, k > 0
-    neighbours = [
-        ((i, right), has_right), ((i, left), has_left),
-        ((up, right), has_up & has_right), ((up, left), has_up & has_left),
-        ((down, right), has_down & has_right), ((down, left), has_down & has_left),
-    ]
+    gives_left, gives_right = (i < 2) & has_left, (i >= N_ROW - 2) & has_right
 
     @pl.loop(1, N_ROW)
     def _(step):
         pl.semaphore_signal(barrier, inc=1, device_id=(lax.rem(i + step, N_ROW), k), device_id_type=MESH)
 
-    for device, present in neighbours:
+    for present, column, first in ((has_left, left, N_ROW - 2), (has_right, right, 0)):
         @pl.when(present)
         def _():
-            pl.semaphore_signal(barrier, inc=1, device_id=device, device_id_type=MESH)
+            for j in (first, first + 1):
+                pl.semaphore_signal(barrier, inc=1, device_id=(j, column), device_id_type=MESH)
 
     token_load.wait()
     mine = tokens[...].astype(F32).reshape(192, D).astype(BF16)
     send1[...] = dot(send_selector(), mine).reshape(32, 8, D).astype(BF16)
     recv1[i] = send1[i]
-    across = has_left.astype(I32) + has_right.astype(I32)
-    along = has_down.astype(I32) + has_up.astype(I32)
-    pl.semaphore_wait(barrier, N_ROW - 1 + across * (1 + along))
+    pl.semaphore_wait(barrier, N_ROW - 1 + N_ROW * (gives_left.astype(I32) + gives_right.astype(I32)))
 
     def exchange(source, target, sem):
         @pl.loop(1, N_ROW)
@@ -240,104 +229,144 @@
     x = recv1[...].astype(F32).reshape(256, D)
     block_out = attend_lines(x, gain[...], w_qkv[...], w_out[...])
     send2[...] = block_out.reshape(32, 8, D).astype(BF16)
-    cat[i] = send2[i]
-    exchange(send2, cat, 1)
+    near[i] = send2[i]
+
+    def give(present, column, group, sem):
+        @pl.when(present)
+        def _():
+            @pl.loop(0, N_ROW)
+            def _(step):
+                j = lax.rem(i + step, N_ROW)
+                pltpu.make_async_remote_copy(
+                    src_ref=send2.at[j], dst_ref=near.at[group],
+                    send_sem=halo_send_sem.at[sem], recv_sem=halo_recv_sem.at[sem],
+                    device_id=(j, column), device_id_type=MESH,
+                ).start()
+
+    for row, group, given_to, column, sem in (
+        (N_ROW - 2, 32, has_right, right, 0), (N_ROW - 1, 33, has_right, right, 0),
+        (0, 34, has_left, left, 1), (1, 35, has_left, left, 1),
+    ):
+        give((i == row) & given_to, column, group, sem)
+    exchange(send2, near, 1)
 
     row_sel[...] = row_halo_selector()
     perm[...] = lane_permutation()
     edge_sel[...] = edge_selector()
     for n, da in enumerate((0, -1, 1)):
-        halo_sel[n] = halo_selector(da, i, k)
+        near_sel[n] = near_selector(da)
+        far_sel[n] = far_selector(da)
     shifted[0] = jnp.zeros(shifted.shape[1:], BF16)
     shifted[5] = jnp.zeros(shifted.shape[1:], BF16)
-    for n, size, present in ((32, 8, has_down), (40, 8, has_up)):
-        @pl.when(jnp.logical_not(present))
-        def _():
-            cat[n : n + size] = jnp.zeros((size, 8, D), BF16)
-    sides = [has_left, has_right, has_down & has_left, has_down & has_right, has_up & has_left, has_up & has_right]
-    for n, present in enumerate(sides):
-        @pl.when(jnp.logical_not(present))
-        def _():
-            cat[48 + 2 * n : 50 + 2 * n] = jnp.zeros((2, 8, D), BF16)
-    cat[60:64] = jnp.zeros((4, 8, D), BF16)
+    shifted[1:5, 4:6] = jnp.zeros((4, 2, 16, 3 * D), BF16)
+    near[36:48] = jnp.zeros((12, 8, D), BF16)
+    far[18:32] = jnp.zeros((14, 8, D), BF16)
+
+    @pl.when(jnp.logical_not(has_left))
+    def _():
+        near[32:34] = jnp.zeros((2, 8, D), BF16)
+
+    @pl.when(jnp.logical_not(has_right))
+    def _():
+        near[34:36] = jnp.zeros((2, 8, D), BF16)
+
+    @pl.when(jnp.logical_not(has_down))
+    def _():
+        far[0:9] = jnp.zeros((9, 8, D), BF16)
+
+    @pl.when(jnp.logical_not(has_up))
+    def _():
+        far[9:18] = jnp.zeros((9, 8, D), BF16)
 
     @pl.loop(3, 6)
     def _(q):
         prepare(q)
 
     drain(send1, recv1, N_ROW - 1, 0).wait_send()
-    drain(send2, cat, N_ROW - 1, 1).wait_recv()
-
-    own = cat[:32].astype(F32).reshape(256, D).astype(BF16)
-    row_halo[...] = dot(row_sel[...], own).reshape(16, 8, D).astype(BF16)
-
-    lowest, highest = cat.at[pl.ds(0, 2)], cat.at[pl.ds(30, 2)]
-    halos = [
-        (row_halo.at[pl.ds(0, 8)], 40, (down, k), has_down),
-        (row_halo.at[pl.ds(8, 8)], 32, (up, k), has_up),
-        (lowest, 50, (i, left), has_left),
-        (highest, 48, (i, right), has_right),
-        (highest, 52, (up, right), has_up & has_right),
-        (lowest, 54, (up, left), has_up & has_left),
-        (highest, 56, (down, right), has_down & has_right),
-        (lowest, 58, (down, left), has_down & has_left),
-    ]
-
-    def halo_copy(n):
-        source, at, device, _ = halos[n]
+    drain(send2, near, N_ROW - 1, 1).wait_recv()
+
+    def given(count, group, sem):
         return pltpu.make_async_remote_copy(
-            src_ref=source, dst_ref=cat.at[pl.ds(at, 8 if n < 2 else 2)],
-            send_sem=halo_send_sem.at[n], recv_sem=halo_recv_sem.at[n],
-            device_id=device, device_id_type=MESH,
+            src_ref=send2.at[pl.ds(0, count)], dst_ref=near.at[pl.ds(group, count)],
+            send_sem=halo_send_sem.at[sem], recv_sem=halo_recv_sem.at[sem],
+            device_id=(lax.rem(i + 1, N_ROW), k), device_id_type=MESH,
         )
 
-    for n in range(8):
-        @pl.when(halos[n][3])
-        def _():
-            halo_copy(n).start()
-
-    drain(send2, cat, N_ROW - 1, 1).wait_send()
-    arrives = [has_up, has_down, has_right, has_left, has_down & has_left, has_down & has_right, has_up & has_left, has_up & has_right]
-    for n in range(8):
-        @pl.when(arrives[n])
-        def _():
-            halo_copy(n).wait_recv()
-
-        @pl.when(halos[n][3])
-        def _():
-            halo_copy(n).wait_send()
-
-
-    gathered = cat[...].astype(F32).reshape(512, D).astype(BF16)
+    @pl.when(has_left)
+    def _():
+        given(2, 32, 0).wait_recv()
+
+    @pl.when(has_right)
+    def _():
+        given(2, 34, 1).wait_recv()
+
+    gathered = near[...].astype(F32).reshape(384, D).astype(BF16)
+    row_halo[...] = dot(row_sel[...], gathered).reshape(18, 8, D).astype(BF16)
+
+    def row_copy(n):
+        return pltpu.make_async_remote_copy(
+            src_ref=row_halo.at[pl.ds(9 * n, 9)], dst_ref=far.at[pl.ds(9 - 9 * n, 9)],
+            send_sem=halo_send_sem.at[2 + n], recv_sem=halo_recv_sem.at[2 + n],
+            device_id=(up if n else down, k), device_id_type=MESH,
+        )
+
+    @pl.when(has_down)
+    def _():
+        row_copy(0).start()
+
+    @pl.when(has_up)
+    def _():
+        row_copy(1).start()
+
     for n in range(3):
-        picked = dot(halo_sel[n], gathered).reshape(4, 6, 16, D).astype(BF16)
-        shifted[1:5, :, :, n * D : (n + 1) * D] = picked
-
+        picked = dot(near_sel[n], gathered).reshape(4, 3, 16, D).astype(BF16)
+        shifted[1:5, 1:4, :, n * D : (n + 1) * D] = picked
     spans = ((0, 0, 8, 2), (-1, 0, 2, 10), (1, 6, 2, 0))
-
     for dz, z, n, kz in spans:
-        pairs = pl.ds(kz // 2, n // 2)
         here = pl.ds(1 + dz, 4)
         level = pl.ds(z, n)
-        for part in range(3):
-            token_part = shifted[here, 1:5, :, part * D : (part + 1) * D].reshape(256, D)
-            if part == 0:
-                rows, size, y = main_w[:, :, pairs], 8, 0
-            else:
-                rows, size, y = side_w[part - 1, :, :, pairs], 2, 6 * (part - 1)
-            found = dot_nt(rows.reshape(-1, D), token_part).reshape(4, size, n, 8, 256)
-            if dz == 0 and part == 0:
-                acc[...] = found
-            else:
-                acc[:, pl.ds(y, size), level] += found
+        pairs = pl.ds(kz // 2, n // 2)
+        token_part = shifted[here, 1:5, :, :D].reshape(256, D)
+        found = dot_nt(main_w[:, :, pairs].reshape(-1, D), token_part).reshape(4, 8, n, 8, 256)
+        if dz == 0:
+            acc[...] = found
+        else:
+            acc[:, :, level] += found
         for side in range(2):
-            token_part = shifted[here, pl.ds(2 * side, 4)].reshape(256, 3 * D)
-            rows = edge_w[side, :, pl.ds(kz, n)].reshape(-1, 3 * D)
+            token_part = shifted[here, 1:5, :, (side + 1) * D : (side + 2) * D].reshape(256, D)
+            rows = side_w[side, :, :, pairs].reshape(-1, D)
+            acc[:, pl.ds(6 * side, 2), level] += dot_nt(rows, token_part).reshape(4, 2, n, 8, 256)
+
+    drain(send2, near, N_ROW - 1, 1).wait_send()
+    for present, sem in ((gives_right, 0), (gives_left, 1)):
+        @pl.when(present)
+        def _():
+            given(N_ROW, 0, sem).wait_send()
+
+    for sends, comes, n in ((has_down, has_up, 0), (has_up, has_down, 1)):
+        @pl.when(sends)
+        def _():
+            row_copy(n).wait_send()
+
+        @pl.when(comes)
+        def _():
+            row_copy(n).wait_recv()
+
+    gathered = far[...].astype(F32).reshape(256, D).astype(BF16)
+    for n in range(3):
+        picked = dot(far_sel[n], gathered).reshape(4, 2, 16, D).astype(BF16)
+        shifted[1:5, 0, :, n * D : (n + 1) * D] = picked[:, 0]
+        shifted[1:5, 4, :, n * D : (n + 1) * D] = picked[:, 1]
+
+    for dz, z, n, kz in spans:
+        for side in range(2):
+            token_part = shifted[1 + dz : 5 + dz, 2 * side : 2 * side + 4].reshape(256, 3 * D)
+            rows = edge_w[side, :, kz : kz + n].reshape(-1, 3 * D)
             found = dot_nt(rows, token_part).reshape(4, n, 16, 256)
             if dz == 0:
                 edge_acc[:, :, side] = found
             else:
-                edge_acc[:, level, side] += found
+                edge_acc[:, z : z + n, side] += found
     for c in range(4):
         edges = edge_acc[c].reshape(256, 256).astype(BF16)
         total = acc[c].reshape(512, 256) + dot(edge_sel[...], edges)
@@ -376,16 +405,18 @@
             pltpu.VMEM((32, 8, D), BF16),
             pltpu.VMEM((32, 8, D), BF16),
             pltpu.VMEM((32, 8, D), BF16),
-            pltpu.VMEM((64, 8, D), BF16),
-            pltpu.VMEM((16, 8, D), BF16),
+            pltpu.VMEM((48, 8, D), BF16),
+            pltpu.VMEM((32, 8, D), BF16),
+            pltpu.VMEM((18, 8, D), BF16),
             pltpu.VMEM((8, 192, 256), BF16),
             pltpu.VMEM((4, 8, 6, 16, D), BF16),
             pltpu.VMEM((2, 4, 2, 6, 16, D), BF16),
             pltpu.VMEM((2, 4, 12, 16, 3 * D), BF16),
-            pltpu.VMEM((3, 384, 512), BF16),
+            pltpu.VMEM((3, 192, 384), BF16),
+            pltpu.VMEM((3, 128, 256), BF16),
             pltpu.VMEM((1024, 768), BF16),
             pltpu.VMEM((512, 256), BF16),
-            pltpu.VMEM((128, 256), BF16),
+            pltpu.VMEM((144, 384), BF16),
             pltpu.VMEM((6, 6, 16, 3 * D), BF16),
             pltpu.VMEM((4, 8, 8, 8, 256), F32),
             pltpu.VMEM((4, 8, 2, 16, 256), F32),
@@ -393,8 +424,8 @@
             pltpu.SemaphoreType.DMA((11,)),
             pltpu.SemaphoreType.DMA((2,)),
             pltpu.SemaphoreType.DMA((2,)),
-            pltpu.SemaphoreType.DMA((8,)),
-            pltpu.SemaphoreType.DMA((8,)),
+            pltpu.SemaphoreType.DMA((4,)),
+            pltpu.SemaphoreType.DMA((4,)),
         ],
         compiler_params=pltpu.CompilerParams(
             collective_id=0, has_side_effects=True, vmem_limit_bytes=60 * 1024 * 1024

time: 41.5 us -> 40.7 us (0.981)
  the two profiles are of different devices: /device:TPU:7 before, /device:TPU:1 now
where the time goes in v4:
time: 40.7 us; the launch traced here: 40.6 us
  Pallas kernels  38.5 us (95%)
  local copies, waits for them, and re-layouts  2.09 us (5%)
    pallas_call x1, Pallas kernels, body(): pl.pallas_call(kernel, out_shape=jax.ShapeDtypeStruct((4, 32, 24, 128), B...  38.5 us
    unnamed x1, local copies, waits for them, and re-layouts  2.09 us

profile of v4, /device:TPU:1, one launch (start us, length us, event | category | flops | bytes accessed | tf_op | source)
XLA Modules:
  0.0 40.6 jit_solution(16397922156174210661)
XLA Ops:
  0.0 38.5 %airflow_block.1 = bf16[4,32,24,128]{3,2,1,0:T(8,128)(2,1)} custom-call(bf16[3,16,4,512]{3,2,1,0:T(4,128)(2,1)} %tokens_hbm.1, f32[1,512]{1,0:T(1,128)} %bitcast.1, bf16[512,1536]{1,0:T(8,128)(2,1)} %w_qkv_hbm.1, bf16[512,512]{1,0:T(8,128)(2,1)} %w_out_hbm.1, bf16[512,6912]{1,0:T(8,128)(2,1)} %w_rec_hbm.1, s32[24,128]{1,0:T(8,128)} %solid_hbm.1), custom_call_target="tpu_custom_call" | custom-call | flops 6000000000 | bytes 11000000 | tf_op jit(solution)/shard_map/airflow_block/pallas_call | solution.py:393
  38.5 2.1 %copy.8 = bf16[4,32,24,128]{3,2,1,0:T(8,128)(2,1)} copy(bf16[4,32,24,128]{3,2,1,0:T(8,128)(2,1)} %airflow_block.1) | data formatting | bytes 1572864

commit v5 on v4

--- a/solution.py
+++ b/solution.py
@@ -30,7 +30,8 @@
 
 def send_selector():
     row = iota((256, 1), 0)
-    source = (row & 3) * 64 + (row >> 3) * 2 + ((row >> 2) & 1)
+    pair = ((row >> 3) & 15) * 2 + (row >> 7)
+    source = (row & 3) * 64 + pair * 2 + ((row >> 2) & 1)
     source = jnp.where((row & 3) < 3, source, -1)
     return one_hot(iota((256, 192), 1) == source)
 
@@ -157,16 +158,17 @@
     up, down = lax.rem(i + 1, N_ROW), lax.rem(i + N_ROW - 1, N_ROW)
     right, left = lax.rem(k + 1, N_AISLE), lax.rem(k + N_AISLE - 1, N_AISLE)
     has_up, has_down, has_right, has_left = i < N_ROW - 1, i > 0, k < N_AISLE - 1, k > 0
-    gives_left, gives_right = (i < 2) & has_left, (i >= N_ROW - 2) & has_right
+    pair = lax.rem(i, 16) * 2 + lax.div(i, 16)
+    gives_left, gives_right = (lax.rem(i, 16) == 0) & has_left, (lax.rem(i, 16) == 15) & has_right
 
     @pl.loop(1, N_ROW)
     def _(step):
         pl.semaphore_signal(barrier, inc=1, device_id=(lax.rem(i + step, N_ROW), k), device_id_type=MESH)
 
-    for present, column, first in ((has_left, left, N_ROW - 2), (has_right, right, 0)):
+    for present, column, first in ((has_left, left, 15), (has_right, right, 0)):
         @pl.when(present)
         def _():
-            for j in (first, first + 1):
+            for j in (first, first + 16):
                 pl.semaphore_signal(barrier, inc=1, device_id=(j, column), device_id_type=MESH)
 
     token_load.wait()
@@ -175,12 +177,12 @@
     recv1[i] = send1[i]
     pl.semaphore_wait(barrier, N_ROW - 1 + N_ROW * (gives_left.astype(I32) + gives_right.astype(I32)))
 
-    def exchange(source, target, sem):
+    def exchange(source, target, place, sem):
         @pl.loop(1, N_ROW)
         def _(step):
             j = lax.rem(i + step, N_ROW)
             pltpu.make_async_remote_copy(
-                src_ref=source.at[j], dst_ref=target.at[i],
+                src_ref=source.at[j], dst_ref=target.at[place],
                 send_sem=send_sem.at[sem], recv_sem=recv_sem.at[sem],
                 device_id=(j, k), device_id_type=MESH,
             ).start()
@@ -192,7 +194,7 @@
             device_id=(lax.rem(i + 1, N_ROW), k), device_id_type=MESH,
         )
 
-    exchange(send1, recv1, 0)
+    exchange(send1, recv1, i, 0)
 
     @pl.loop(0, 8)
     def _(s):
@@ -229,7 +231,7 @@
     x = recv1[...].astype(F32).reshape(256, D)
     block_out = attend_lines(x, gain[...], w_qkv[...], w_out[...])
     send2[...] = block_out.reshape(32, 8, D).astype(BF16)
-    near[i] = send2[i]
+    near[pair] = send2[i]
 
     def give(present, column, group, sem):
         @pl.when(present)
@@ -244,11 +246,11 @@
                 ).start()
 
     for row, group, given_to, column, sem in (
-        (N_ROW - 2, 32, has_right, right, 0), (N_ROW - 1, 33, has_right, right, 0),
-        (0, 34, has_left, left, 1), (1, 35, has_left, left, 1),
+        (15, 32, has_right, right, 0), (31, 33, has_right, right, 0),
+        (0, 34, has_left, left, 1), (16, 35, has_left, left, 1),
     ):
         give((i == row) & given_to, column, group, sem)
-    exchange(send2, near, 1)
+    exchange(send2, near, pair, 1)
 
     row_sel[...] = row_halo_selector()
     perm[...] = lane_permutation()

time: 40.7 us -> 39.5 us (0.971)
  the two profiles are of different devices: /device:TPU:1 before, /device:TPU:7 now
where the time goes in v5:
time: 39.5 us; the launch traced here: 38.7 us
  Pallas kernels  36.6 us (93%)
  local copies, waits for them, and re-layouts  2.09 us (5%)
    pallas_call x1, Pallas kernels, body(): pl.pallas_call(kernel, out_shape=jax.ShapeDtypeStruct((4, 32, 24, 128), B...  36.6 us
    unnamed x1, local copies, waits for them, and re-layouts  2.09 us

profile of v5, /device:TPU:7, one launch (start us, length us, event | category | flops | bytes accessed | tf_op | source)
XLA Modules:
  0.0 38.7 jit_solution(10015268692604125640)
XLA Ops:
  0.0 36.6 %airflow_block.1 = bf16[4,32,24,128]{3,2,1,0:T(8,128)(2,1)} custom-call(bf16[3,16,4,512]{3,2,1,0:T(4,128)(2,1)} %tokens_hbm.1, f32[1,512]{1,0:T(1,128)} %bitcast.1, bf16[512,1536]{1,0:T(8,128)(2,1)} %w_qkv_hbm.1, bf16[512,512]{1,0:T(8,128)(2,1)} %w_out_hbm.1, bf16[512,6912]{1,0:T(8,128)(2,1)} %w_rec_hbm.1, s32[24,128]{1,0:T(8,128)} %solid_hbm.1), custom_call_target="tpu_custom_call" | custom-call | flops 6000000000 | bytes 11000000 | tf_op jit(solution)/shard_map/airflow_block/pallas_call | solution.py:395
  36.6 2.1 %copy.8 = bf16[4,32,24,128]{3,2,1,0:T(8,128)(2,1)} copy(bf16[4,32,24,128]{3,2,1,0:T(8,128)(2,1)} %airflow_block.1) | data formatting | bytes 1572864

commit v6 on v5

--- a/solution.py
+++ b/solution.py
@@ -119,8 +119,8 @@
             scores = dot_nt(query * mask, key) * (1.0 / 8.0)
             scores = jnp.where(valid, scores, -jnp.inf)
             grown = jnp.exp(scores - jnp.max(scores, axis=-1, keepdims=True))
-            weights = grown / jnp.sum(grown, axis=-1, keepdims=True)
-            halves.append(dot(weights.astype(BF16), value))
+            total = jnp.sum(grown, axis=-1, keepdims=True)
+            halves.append(dot(grown.astype(BF16), value) / total)
         parts.append(jnp.where(first, halves[0], halves[1]).astype(BF16))
     attended = jnp.concatenate(parts, axis=1)
     return x + dot(attended, w_out)
@@ -258,9 +258,7 @@
     for n, da in enumerate((0, -1, 1)):
         near_sel[n] = near_selector(da)
         far_sel[n] = far_selector(da)
-    shifted[0] = jnp.zeros(shifted.shape[1:], BF16)
-    shifted[5] = jnp.zeros(shifted.shape[1:], BF16)
-    shifted[1:5, 4:6] = jnp.zeros((4, 2, 16, 3 * D), BF16)
+    shifted[:, 4:6] = jnp.zeros((4, 2, 16, 3 * D), BF16)
     near[36:48] = jnp.zeros((12, 8, D), BF16)
     far[18:32] = jnp.zeros((14, 8, D), BF16)
 
@@ -322,22 +320,26 @@
 
     for n in range(3):
         picked = dot(near_sel[n], gathered).reshape(4, 3, 16, D).astype(BF16)
-        shifted[1:5, 1:4, :, n * D : (n + 1) * D] = picked
-    spans = ((0, 0, 8, 2), (-1, 0, 2, 10), (1, 6, 2, 0))
-    for dz, z, n, kz in spans:
-        here = pl.ds(1 + dz, 4)
-        level = pl.ds(z, n)
-        pairs = pl.ds(kz // 2, n // 2)
-        token_part = shifted[here, 1:5, :, :D].reshape(256, D)
-        found = dot_nt(main_w[:, :, pairs].reshape(-1, D), token_part).reshape(4, 8, n, 8, 256)
-        if dz == 0:
-            acc[...] = found
-        else:
-            acc[:, :, level] += found
-        for side in range(2):
-            token_part = shifted[here, 1:5, :, (side + 1) * D : (side + 2) * D].reshape(256, D)
-            rows = side_w[side, :, :, pairs].reshape(-1, D)
-            acc[:, pl.ds(6 * side, 2), level] += dot_nt(rows, token_part).reshape(4, 2, n, 8, 256)
+        shifted[:, 1:4, :, n * D : (n + 1) * D] = picked
+    lane = iota((1, 256), 1)
+
+    def from_below(values):
+        return jnp.where(lane >= 64, pltpu.roll(values.reshape(-1, 256), 64, 1), 0.0).reshape(values.shape)
+
+    def from_above(values):
+        return jnp.where(lane < 192, pltpu.roll(values.reshape(-1, 256), 192, 1), 0.0).reshape(values.shape)
+
+    found = dot_nt(main_w[...].reshape(-1, D), shifted[:, 1:5, :, :D].reshape(256, D)).reshape(4, 8, 12, 8, 256)
+    acc[...] = found[:, :, 2:10]
+    acc[:, :, 0:2] += from_below(found[:, :, 10:12])
+    acc[:, :, 6:8] += from_above(found[:, :, 0:2])
+    for side in range(2):
+        token_part = shifted[:, 1:5, :, (side + 1) * D : (side + 2) * D].reshape(256, D)
+        found = dot_nt(side_w[side].reshape(-1, D), token_part).reshape(4, 2, 12, 8, 256)
+        rows = pl.ds(6 * side, 2)
+        acc[:, rows] += found[:, :, 2:10]
+        acc[:, rows, 0:2] += from_below(found[:, :, 10:12])
+        acc[:, rows, 6:8] += from_above(found[:, :, 0:2])
 
     drain(send2, near, N_ROW - 1, 1).wait_send()
     for present, sem in ((gives_right, 0), (gives_left, 1)):
@@ -357,36 +359,36 @@
     gathered = far[...].astype(F32).reshape(256, D).astype(BF16)
     for n in range(3):
         picked = dot(far_sel[n], gathered).reshape(4, 2, 16, D).astype(BF16)
-        shifted[1:5, 0, :, n * D : (n + 1) * D] = picked[:, 0]
-        shifted[1:5, 4, :, n * D : (n + 1) * D] = picked[:, 1]
-
-    for dz, z, n, kz in spans:
-        for side in range(2):
-            token_part = shifted[1 + dz : 5 + dz, 2 * side : 2 * side + 4].reshape(256, 3 * D)
-            rows = edge_w[side, :, kz : kz + n].reshape(-1, 3 * D)
-            found = dot_nt(rows, token_part).reshape(4, n, 16, 256)
-            if dz == 0:
-                edge_acc[:, :, side] = found
-            else:
-                edge_acc[:, z : z + n, side] += found
-    for c in range(4):
-        edges = edge_acc[c].reshape(256, 256).astype(BF16)
-        total = acc[c].reshape(512, 256) + dot(edge_sel[...], edges)
-        total = total.astype(BF16)
-        for y in range(8):
+        shifted[:, 0, :, n * D : (n + 1) * D] = picked[:, 0]
+        shifted[:, 4, :, n * D : (n + 1) * D] = picked[:, 1]
+
+    for side in range(2):
+        token_part = shifted[:, 2 * side : 2 * side + 4].reshape(256, 3 * D)
+        found = dot_nt(edge_w[side].reshape(-1, 3 * D), token_part).reshape(4, 12, 16, 256)
+        edge_acc[:, :, side] = found[:, 2:10]
+        edge_acc[:, 0:2, side] += from_below(found[:, 10:12])
+        edge_acc[:, 6:8, side] += from_above(found[:, 0:2])
+
+    solid = solid_ref[...]
+    insides = [iota((8, 24, 128), 0) + 8 * h < solid[None] for h in range(4)]
+    for first_c in range(0, 4, 2):
+        lines = []
+        for c in range(first_c, first_c + 2):
+            edges = edge_acc[c].reshape(256, 256).astype(BF16)
+            total = acc[c].reshape(512, 256) + dot(edge_sel[...], edges)
             for b in range(2):
-                ready[b, c, :, y * 128 : (y + 1) * 128] = total[y * 64 : (y + 1) * 64, b * 128 : (b + 1) * 128]
-    solid = solid_ref[...]
-    for low in range(2):
-        cells = dot(ready[...].reshape(512, 1024), perm[:, low * 384 : (low + 1) * 384])
-        for b in range(2):
-            h = 2 * b + low
-            part = cells[b * 256 : (b + 1) * 256]
-            part = jnp.concatenate(
-                [part[:, r * 128 : (r + 1) * 128].reshape(4, 8, 8, 128) for r in range(3)], axis=2
-            )
-            level = iota((4, 8, 24, 128), 1) + 8 * h
-            out_ref[:, 8 * h : 8 * h + 8] = jnp.where(level < solid[None, None], 0.0, part).astype(BF16)
+                lines.append(jnp.concatenate(
+                    [total[y * 64 : (y + 1) * 64, b * 128 : (b + 1) * 128] for y in range(8)], axis=1
+                ))
+        cells = dot(jnp.concatenate(lines, axis=0).astype(BF16), perm[...])
+        for n in range(2):
+            for h in range(4):
+                b, low = h // 2, h % 2
+                part = cells[128 * n + b * 64 : 128 * n + (b + 1) * 64]
+                part = jnp.concatenate(
+                    [part[:, low * 384 + r * 128 : low * 384 + (r + 1) * 128].reshape(8, 8, 128) for r in range(3)], axis=1
+                )
+                out_ref[first_c + n, 8 * h : 8 * h + 8] = jnp.where(insides[h], 0.0, part).astype(BF16)
 
 
 def body(tokens, ln_gain, w_qkv, w_out, w_rec, solid_top):
@@ -419,7 +421,7 @@
             pltpu.VMEM((1024, 768), BF16),
             pltpu.VMEM((512, 256), BF16),
             pltpu.VMEM((144, 384), BF16),
-            pltpu.VMEM((6, 6, 16, 3 * D), BF16),
+            pltpu.VMEM((4, 6, 16, 3 * D), BF16),
             pltpu.VMEM((4, 8, 8, 8, 256), F32),
             pltpu.VMEM((4, 8, 2, 16, 256), F32),
             pltpu.VMEM((2, 4, 64, 1024), BF16),

time: 39.5 us -> 37.6 us (0.952)
  the two profiles are of different devices: /device:TPU:7 before, /device:TPU:1 now
where the time goes in v6:
time: 37.6 us; the launch traced here: 37.5 us
  Pallas kernels  35.4 us (94%)
  local copies, waits for them, and re-layouts  2.09 us (6%)
    pallas_call x1, Pallas kernels, body(): pl.pallas_call(kernel, out_shape=jax.ShapeDtypeStruct((4, 32, 24, 128), B...  35.4 us
    unnamed x1, local copies, waits for them, and re-layouts  2.09 us

profile of v6, /device:TPU:1, one launch (start us, length us, event | category | flops | bytes accessed | tf_op | source)
XLA Modules:
  0.0 37.5 jit_solution(11802553814314595078)
XLA Ops:
  0.0 35.4 %airflow_block.1 = bf16[4,32,24,128]{3,2,1,0:T(8,128)(2,1)} custom-call(bf16[3,16,4,512]{3,2,1,0:T(4,128)(2,1)} %tokens_hbm.1, f32[1,512]{1,0:T(1,128)} %bitcast.1, bf16[512,1536]{1,0:T(8,128)(2,1)} %w_qkv_hbm.1, bf16[512,512]{1,0:T(8,128)(2,1)} %w_out_hbm.1, bf16[512,6912]{1,0:T(8,128)(2,1)} %w_rec_hbm.1, s32[24,128]{1,0:T(8,128)} %solid_hbm.1), custom_call_target="tpu_custom_call" | custom-call | flops 6000000000 | bytes 11000000 | tf_op jit(solution)/shard_map/airflow_block/pallas_call | solution.py:397
  35.4 2.1 %copy.8 = bf16[4,32,24,128]{3,2,1,0:T(8,128)(2,1)} copy(bf16[4,32,24,128]{3,2,1,0:T(8,128)(2,1)} %airflow_block.1) | data formatting | bytes 1572864

commit v7 on v6

--- a/solution.py
+++ b/solution.py
@@ -61,19 +61,25 @@
 
 
 def near_selector(da):
-    q = iota((192, 1), 0)
-    h = jnp.where(q >= 144, 3, jnp.where(q >= 96, 2, jnp.where(q >= 48, 1, 0)))
-    rest = q - 48 * h
-    r, a = rest >> 4, (rest & 15) + da
+    q = iota((256, 1), 0)
+    h, r, a = q >> 6, (q >> 4) & 3, (q & 15) + da
     block = jnp.where(a < 0, 16, jnp.where(a > 15, 17, a))
-    return one_hot(iota((192, 384), 1) == block * 16 + h * 4 + r)
+    return one_hot(iota((256, 384), 1) == block * 16 + h * 4 + r)
 
 
 def far_selector(da):
-    q = iota((128, 1), 0)
-    h, side, a = q >> 5, (q >> 4) & 1, (q & 15) + da
+    q = iota((64, 1), 0)
+    h, a = q >> 4, (q & 15) + da
     block = jnp.where(a < 0, 16, jnp.where(a > 15, 17, a))
-    return one_hot(iota((128, 256), 1) == side * 72 + block * 4 + h)
+    return one_hot(iota((64, 128), 1) == block * 4 + h)
+
+
+def slot_selector():
+    row = iota((256, 1), 0)
+    i, slot = row >> 3, row & 3
+    beside = jnp.where((i & 1) == 0, row - 9, row + 5)
+    beside = jnp.where((i == 0) | (i == N_ROW - 1), -1, beside)
+    return one_hot(iota((256, 256), 1) == jnp.where(slot < 3, row, beside))
 
 
 def lane_permutation():
@@ -92,10 +98,10 @@
     return one_hot(iota((512, 256), 0) == target)
 
 
-def row_halo_selector():
-    row = iota((144, 1), 0)
-    source = jnp.where(row >= 72, (row - 72) * 4 + 2, row * 4)
-    return one_hot(iota((144, 384), 1) == source)
+def row_halo_selector(core):
+    row = iota((80, 1), 0)
+    source = jnp.where(row < 72, row * 4 + 2 - 2 * core, -1)
+    return one_hot(iota((80, 384), 1) == source)
 
 
 def attend_lines(x, gain, w_qkv, w_out):
@@ -130,7 +136,7 @@
     tokens_hbm, gain_hbm, w_qkv_hbm, w_out_hbm, w_rec_hbm, solid_hbm,
     out_ref,
     tokens, gain, solid_ref, w_qkv, w_out, w_rec, send1, recv1, send2, near, far, row_halo,
-    w_sel, main_w, side_w, edge_w, near_sel, far_sel, perm, edge_sel, row_sel,
+    w_sel, main_w, side_w, edge_w, near_sel, far_sel, perm, edge_sel, row_sel, slot_sel,
     shifted, acc, edge_acc, ready,
     load_sem, send_sem, recv_sem, halo_send_sem, halo_recv_sem,
 ):
@@ -155,9 +161,10 @@
         rec_load(q).start()
 
     barrier = pltpu.get_barrier_semaphore()
-    up, down = lax.rem(i + 1, N_ROW), lax.rem(i + N_ROW - 1, N_ROW)
+    core = lax.rem(i, 2)
+    partner = i + 1 - 2 * core
     right, left = lax.rem(k + 1, N_AISLE), lax.rem(k + N_AISLE - 1, N_AISLE)
-    has_up, has_down, has_right, has_left = i < N_ROW - 1, i > 0, k < N_AISLE - 1, k > 0
+    has_right, has_left = k < N_AISLE - 1, k > 0
     pair = lax.rem(i, 16) * 2 + lax.div(i, 16)
     gives_left, gives_right = (lax.rem(i, 16) == 0) & has_left, (lax.rem(i, 16) == 15) & has_right
 
@@ -220,6 +227,8 @@
                         at = 96 + 48 * side + 16 * part
                         edge_w[side, c, 2 * pair + n, :, part * D : (part + 1) * D] = found[n][at : at + 16].astype(BF16)
 
+    slot_sel[...] = slot_selector()
+
     @pl.loop(0, 3)
     def _(q):
         prepare(q)
@@ -230,7 +239,7 @@
 
     x = recv1[...].astype(F32).reshape(256, D)
     block_out = attend_lines(x, gain[...], w_qkv[...], w_out[...])
-    send2[...] = block_out.reshape(32, 8, D).astype(BF16)
+    send2[...] = dot(slot_sel[...], block_out.astype(BF16)).reshape(32, 8, D).astype(BF16)
     near[pair] = send2[i]
 
     def give(present, column, group, sem):
@@ -252,7 +261,7 @@
         give((i == row) & given_to, column, group, sem)
     exchange(send2, near, pair, 1)
 
-    row_sel[...] = row_halo_selector()
+    row_sel[...] = row_halo_selector(core)
     perm[...] = lane_permutation()
     edge_sel[...] = edge_selector()
     for n, da in enumerate((0, -1, 1)):
@@ -260,7 +269,7 @@
         far_sel[n] = far_selector(da)
     shifted[:, 4:6] = jnp.zeros((4, 2, 16, 3 * D), BF16)
     near[36:48] = jnp.zeros((12, 8, D), BF16)
-    far[18:32] = jnp.zeros((14, 8, D), BF16)
+    far[9:16] = jnp.zeros((7, 8, D), BF16)
 
     @pl.when(jnp.logical_not(has_left))
     def _():
@@ -269,14 +278,6 @@
     @pl.when(jnp.logical_not(has_right))
     def _():
         near[34:36] = jnp.zeros((2, 8, D), BF16)
-
-    @pl.when(jnp.logical_not(has_down))
-    def _():
-        far[0:9] = jnp.zeros((9, 8, D), BF16)
-
-    @pl.when(jnp.logical_not(has_up))
-    def _():
-        far[9:18] = jnp.zeros((9, 8, D), BF16)
 
     @pl.loop(3, 6)
     def _(q):
@@ -301,26 +302,18 @@
         given(2, 34, 1).wait_recv()
 
     gathered = near[...].astype(F32).reshape(384, D).astype(BF16)
-    row_halo[...] = dot(row_sel[...], gathered).reshape(18, 8, D).astype(BF16)
-
-    def row_copy(n):
-        return pltpu.make_async_remote_copy(
-            src_ref=row_halo.at[pl.ds(9 * n, 9)], dst_ref=far.at[pl.ds(9 - 9 * n, 9)],
-            send_sem=halo_send_sem.at[2 + n], recv_sem=halo_recv_sem.at[2 + n],
-            device_id=(up if n else down, k), device_id_type=MESH,
-        )
-
-    @pl.when(has_down)
-    def _():
-        row_copy(0).start()
-
-    @pl.when(has_up)
-    def _():
-        row_copy(1).start()
+    row_halo[...] = dot(row_sel[...], gathered).reshape(10, 8, D).astype(BF16)
+    row_copy = pltpu.make_async_remote_copy(
+        src_ref=row_halo.at[pl.ds(0, 9)], dst_ref=far.at[pl.ds(0, 9)],
+        send_sem=halo_send_sem.at[2], recv_sem=halo_recv_sem.at[2],
+        device_id=(partner, k), device_id_type=MESH,
+    )
+    row_copy.start()
 
     for n in range(3):
-        picked = dot(near_sel[n], gathered).reshape(4, 3, 16, D).astype(BF16)
-        shifted[:, 1:4, :, n * D : (n + 1) * D] = picked
+        picked = dot(near_sel[n], gathered).reshape(4, 4, 16, D).astype(BF16)
+        shifted[:, 1:4, :, n * D : (n + 1) * D] = picked[:, 0:3]
+        shifted[:, pl.ds(4 * core, 1), :, n * D : (n + 1) * D] = picked[:, 3:4]
     lane = iota((1, 256), 1)
 
     def from_below(values):
@@ -347,20 +340,12 @@
         def _():
             given(N_ROW, 0, sem).wait_send()
 
-    for sends, comes, n in ((has_down, has_up, 0), (has_up, has_down, 1)):
-        @pl.when(sends)
-        def _():
-            row_copy(n).wait_send()
-
-        @pl.when(comes)
-        def _():
-            row_copy(n).wait_recv()
-
-    gathered = far[...].astype(F32).reshape(256, D).astype(BF16)
+    row_copy.wait()
+
+    gathered = far[...].astype(F32).reshape(128, D).astype(BF16)
     for n in range(3):
-        picked = dot(far_sel[n], gathered).reshape(4, 2, 16, D).astype(BF16)
-        shifted[:, 0, :, n * D : (n + 1) * D] = picked[:, 0]
-        shifted[:, 4, :, n * D : (n + 1) * D] = picked[:, 1]
+        picked = dot(far_sel[n], gathered).reshape(4, 1, 16, D).astype(BF16)
+        shifted[:, pl.ds(4 - 4 * core, 1), :, n * D : (n + 1) * D] = picked
 
     for side in range(2):
         token_part = shifted[:, 2 * side : 2 * side + 4].reshape(256, 3 * D)
@@ -410,17 +395,18 @@
             pltpu.VMEM((32, 8, D), BF16),
             pltpu.VMEM((32, 8, D), BF16),
             pltpu.VMEM((48, 8, D), BF16),
-            pltpu.VMEM((32, 8, D), BF16),
-            pltpu.VMEM((18, 8, D), BF16),
+            pltpu.VMEM((16, 8, D), BF16),
+            pltpu.VMEM((10, 8, D), BF16),
             pltpu.VMEM((8, 192, 256), BF16),
             pltpu.VMEM((4, 8, 6, 16, D), BF16),
             pltpu.VMEM((2, 4, 2, 6, 16, D), BF16),
             pltpu.VMEM((2, 4, 12, 16, 3 * D), BF16),
-            pltpu.VMEM((3, 192, 384), BF16),
-            pltpu.VMEM((3, 128, 256), BF16),
+            pltpu.VMEM((3, 256, 384), BF16),
+            pltpu.VMEM((3, 64, 128), BF16),
             pltpu.VMEM((1024, 768), BF16),
             pltpu.VMEM((512, 256), BF16),
-            pltpu.VMEM((144, 384), BF16),
+            pltpu.VMEM((80, 384), BF16),
+            pltpu.VMEM((256, 256), BF16),
             pltpu.VMEM((4, 6, 16, 3 * D), BF16),
             pltpu.VMEM((4, 8, 8, 8, 256), F32),
             pltpu.VMEM((4, 8, 2, 16, 256), F32),

time: 37.6 us -> 37.8 us (level)
  the two profiles are of different devices: /device:TPU:1 before, /device:TPU:7 now
where the time goes in v7:
time: 37.8 us; the launch traced here: 37.2 us
  Pallas kernels  35.1 us (93%)
  local copies, waits for them, and re-layouts  2.09 us (6%)
    pallas_call x1, Pallas kernels, body(): pl.pallas_call(kernel, out_shape=jax.ShapeDtypeStruct((4, 32, 24, 128), B...  35.1 us
    unnamed x1, local copies, waits for them, and re-layouts  2.09 us

profile of v7, /device:TPU:7, one launch (start us, length us, event | category | flops | bytes accessed | tf_op | source)
XLA Modules:
  0.0 37.2 jit_solution(62063448932348154)
XLA Ops:
  0.0 35.1 %airflow_block.1 = bf16[4,32,24,128]{3,2,1,0:T(8,128)(2,1)} custom-call(bf16[3,16,4,512]{3,2,1,0:T(4,128)(2,1)} %tokens_hbm.1, f32[1,512]{1,0:T(1,128)} %bitcast.1, bf16[512,1536]{1,0:T(8,128)(2,1)} %w_qkv_hbm.1, bf16[512,512]{1,0:T(8,128)(2,1)} %w_out_hbm.1, bf16[512,6912]{1,0:T(8,128)(2,1)} %w_rec_hbm.1, s32[24,128]{1,0:T(8,128)} %solid_hbm.1), custom_call_target="tpu_custom_call" | custom-call | flops 6000000000 | bytes 11000000 | tf_op jit(solution)/shard_map/airflow_block/pallas_call | solution.py:382
  35.1 2.1 %copy.8 = bf16[4,32,24,128]{3,2,1,0:T(8,128)(2,1)} copy(bf16[4,32,24,128]{3,2,1,0:T(8,128)(2,1)} %airflow_block.1) | data formatting | bytes 1572864

commit v8 on v7

--- a/solution.py
+++ b/solution.py
@@ -254,12 +254,12 @@
                     device_id=(j, column), device_id_type=MESH,
                 ).start()
 
+    exchange(send2, near, pair, 1)
     for row, group, given_to, column, sem in (
         (15, 32, has_right, right, 0), (31, 33, has_right, right, 0),
         (0, 34, has_left, left, 1), (16, 35, has_left, left, 1),
     ):
         give((i == row) & given_to, column, group, sem)
-    exchange(send2, near, pair, 1)
 
     row_sel[...] = row_halo_selector(core)
     perm[...] = lane_permutation()

time: 37.8 us -> 37.2 us (0.984); the launches traced: 37.2 us -> 37.1 us
  no operation moved by 1% of the time
where the time goes in v8:
time: 37.2 us; the launch traced here: 37.1 us
  Pallas kernels  35 us (94%)
  local copies, waits for them, and re-layouts  2.09 us (6%)
    pallas_call x1, Pallas kernels, body(): pl.pallas_call(kernel, out_shape=jax.ShapeDtypeStruct((4, 32, 24, 128), B...  35 us
    unnamed x1, local copies, waits for them, and re-layouts  2.09 us

profile of v8, /device:TPU:7, one launch (start us, length us, event | category | flops | bytes accessed | tf_op | source)
XLA Modules:
  0.0 37.1 jit_solution(17968372796796323799)
XLA Ops:
  0.0 35.0 %airflow_block.1 = bf16[4,32,24,128]{3,2,1,0:T(8,128)(2,1)} custom-call(bf16[3,16,4,512]{3,2,1,0:T(4,128)(2,1)} %tokens_hbm.1, f32[1,512]{1,0:T(1,128)} %bitcast.1, bf16[512,1536]{1,0:T(8,128)(2,1)} %w_qkv_hbm.1, bf16[512,512]{1,0:T(8,128)(2,1)} %w_out_hbm.1, bf16[512,6912]{1,0:T(8,128)(2,1)} %w_rec_hbm.1, s32[24,128]{1,0:T(8,128)} %solid_hbm.1), custom_call_target="tpu_custom_call" | custom-call | flops 6000000000 | bytes 11000000 | tf_op jit(solution)/shard_map/airflow_block/pallas_call | solution.py:382
  35.0 2.1 %copy.8 = bf16[4,32,24,128]{3,2,1,0:T(8,128)(2,1)} copy(bf16[4,32,24,128]{3,2,1,0:T(8,128)(2,1)} %airflow_block.1) | data formatting | bytes 1572864

commit v9 on v8

--- a/solution.py
+++ b/solution.py
@@ -138,7 +138,7 @@
     tokens, gain, solid_ref, w_qkv, w_out, w_rec, send1, recv1, send2, near, far, row_halo,
     w_sel, main_w, side_w, edge_w, near_sel, far_sel, perm, edge_sel, row_sel, slot_sel,
     shifted, acc, edge_acc, ready,
-    load_sem, send_sem, recv_sem, halo_send_sem, halo_recv_sem,
+    load_sem, send_sem, recv_sem, halo_send_sem, halo_recv_sem, store_sem, cells_v,
 ):
     i, k = lax.axis_index("row"), lax.axis_index("aisle")
 
@@ -373,17 +373,19 @@
                 part = jnp.concatenate(
                     [part[:, low * 384 + r * 128 : low * 384 + (r + 1) * 128].reshape(8, 8, 128) for r in range(3)], axis=1
                 )
-                out_ref[first_c + n, 8 * h : 8 * h + 8] = jnp.where(insides[h], 0.0, part).astype(BF16)
+                cells_v[first_c + n, 8 * h : 8 * h + 8] = jnp.where(insides[h], 0.0, part).astype(BF16)
+            pltpu.make_async_copy(cells_v.at[first_c + n], out_ref.at[first_c + n], store_sem.at[first_c + n]).start()
+    for c in range(4):
+        pltpu.make_async_copy(cells_v.at[c], out_ref.at[c], store_sem.at[c]).wait()
 
 
 def body(tokens, ln_gain, w_qkv, w_out, w_rec, solid_top):
-    vmem = pl.BlockSpec(memory_space=pltpu.VMEM)
     hbm = pl.BlockSpec(memory_space=pltpu.HBM)
     return pl.pallas_call(
         kernel,
         out_shape=jax.ShapeDtypeStruct((4, 32, 24, 128), BF16),
         in_specs=[hbm] * 6,
-        out_specs=vmem,
+        out_specs=hbm,
         scratch_shapes=[
             pltpu.VMEM((3, 16, 4, D), BF16),
             pltpu.VMEM((1, D), F32),
@@ -416,6 +418,8 @@
             pltpu.SemaphoreType.DMA((2,)),
             pltpu.SemaphoreType.DMA((4,)),
             pltpu.SemaphoreType.DMA((4,)),
+            pltpu.SemaphoreType.DMA((4,)),
+            pltpu.VMEM((4, 32, 24, 128), BF16),
         ],
         compiler_params=pltpu.CompilerParams(
             collective_id=0, has_side_effects=True, vmem_limit_bytes=60 * 1024 * 1024

time: 37.2 us -> 37.1 us (level)
  no operation moved by 1% of the time
where the time goes in v9:
time: 37.1 us; the launch traced here: 37 us
  Pallas kernels  34.9 us (94%)
  local copies, waits for them, and re-layouts  2.09 us (6%)
    pallas_call x1, Pallas kernels, body(): pl.pallas_call(kernel, out_shape=jax.ShapeDtypeStruct((4, 32, 24, 128), B...  34.9 us
    unnamed x1, local copies, waits for them, and re-layouts  2.09 us

profile of v9, /device:TPU:7, one launch (start us, length us, event | category | flops | bytes accessed | tf_op | source)
XLA Modules:
  0.0 37.0 jit_solution(4326278880049600965)
XLA Ops:
  0.0 34.9 %airflow_block.1 = bf16[4,32,24,128]{3,2,1,0:T(8,128)(2,1)} custom-call(bf16[3,16,4,512]{3,2,1,0:T(4,128)(2,1)} %tokens_hbm.1, f32[1,512]{1,0:T(1,128)} %bitcast.1, bf16[512,1536]{1,0:T(8,128)(2,1)} %w_qkv_hbm.1, bf16[512,512]{1,0:T(8,128)(2,1)} %w_out_hbm.1, bf16[512,6912]{1,0:T(8,128)(2,1)} %w_rec_hbm.1, s32[24,128]{1,0:T(8,128)} %solid_hbm.1), custom_call_target="tpu_custom_call" | custom-call | flops 6000000000 | bytes 11000000 | tf_op jit(solution)/shard_map/airflow_block/pallas_call | solution.py:384
  34.9 2.1 %copy.8 = bf16[4,32,24,128]{3,2,1,0:T(8,128)(2,1)} copy(bf16[4,32,24,128]{3,2,1,0:T(8,128)(2,1)} %airflow_block.1) | data formatting | bytes 1572864
